TPU v7x, 32 devices: a whole 2x2x4 slice. The times are simulated.
32 devices in a mesh: section: 2 (over x), seq: 4 (over z), mp: 4 (over y, core).
Axes of the slice: x: 2, y: 2, z: 4, core: 2. Of those that a mesh axis runs over, the one named last changes fastest.
Arguments:
- video: bfloat16 [2, 4, 32, 3072], P(None, None, 'seq'), may hold values from -6 to 6
- text: bfloat16 [2, 32, 3072], P(None, 'seq'), may hold values from -6 to 6
- patch_lengths: int32 [2, 4], replicated, may hold values from 1 to 32, 96 in all within a row
- text_len: int32 [2], replicated, may hold values from 16 to 32, as said below
- timestep: int32 [1], replicated, may hold values from 0 to 999
- w_mod: bfloat16 [2, 512, 9216], P('section', None, 'mp'), may hold values from -0.25 to 0.25
- w_qkv: bfloat16 [2, 3072, 3, 3072], P('section', None, None, 'mp')
- w_out: bfloat16 [2, 3072, 3072], P('section', 'mp'), may hold values from -0.109375 to 0.109375
- stale_cache: bfloat16 [2, 2, 4, 32, 2, 3072], P('section', None, None, 'seq', None, 'mp'), may hold values from -6 to 6
Outputs:
- hidden_video: bfloat16 [2, 2, 4, 32, 3072], P('section', None, None, 'seq')
- hidden_text: bfloat16 [2, 2, 32, 3072], P('section', None, 'seq')
- cache_video: bfloat16 [2, 2, 4, 32, 2, 3072], P('section', None, None, 'seq', None, 'mp')
- cache_text: bfloat16 [2, 2, 32, 2, 3072], P('section', None, 'seq', None, 'mp')
Inputs may be any that keep to these rules, and one draw needn't show every extreme that they name: `patch_lengths`: 4 patch lengths per request summing to 96; in every request the largest is 32. `text_len`: exactly one request has 32, every other fewer.
All inputs are finite; a program needn't handle non-finite values.
Results may differ from a plain program's by a relative error of at most 0.01.
Values may be sent and summed in bfloat16 or wider, within the bound.
A program may use at most 192 MiB of HBM per device.

v0:
```python
import math

import jax
import jax.numpy as jnp
from jax import lax
from jax.sharding import PartitionSpec as P

HEAD = 64


EPS = 1e-05
NEG = -1e30


def passed_along(value, axis, steps):
    count = lax.axis_size(axis)
    leading, last = (max(0, -steps), min(count, count - steps))
    return lax.ppermute(value, axis, [(source, source + steps) for source in range(leading, last)])


def modulation(timestep, weight):
    half_width = weight.shape[0] // 2
    frequency = jnp.exp(-math.log(10000.0) * jnp.arange(half_width, dtype=jnp.float32) / half_width)
    phases = timestep.astype(jnp.float32)[0] * frequency
    embedding = jnp.concatenate([jnp.cos(phases), jnp.sin(phases)])
    active = jax.nn.silu(embedding).astype(jnp.bfloat16)
    return jnp.dot(active[None, :], weight, preferred_element_type=jnp.float32)[0]


def normalize(token_rows, shift_vec, scale_vec):
    values = token_rows.astype(jnp.float32)
    center = values - jnp.mean(values, axis=-1, keepdims=True)
    spread = jnp.mean(center * center, axis=-1, keepdims=True)
    return (center * lax.rsqrt(spread + EPS) * (1.0 + scale_vec) + shift_vec).astype(jnp.bfloat16)


def scores_of(query_heads, key_value, head_count):
    requests, key_count = (key_value.shape[0], key_value.shape[1])
    key_heads = key_value[:, :, 0].reshape(requests, key_count, head_count, HEAD)
    value_heads = key_value[:, :, 1].reshape(requests, key_count, head_count, HEAD)
    scores = jnp.einsum(
        "rqhe,rkhe->rhqk", query_heads, key_heads, preferred_element_type=jnp.float32
    ) * HEAD ** (-0.5)
    return (scores, value_heads)


def masked_max(scores, key_mask):
    return jnp.max(jnp.where(key_mask[:, None, None, :], scores, NEG), axis=-1)


def weighed(scores, key_mask, top_score, value_heads):
    weights = jnp.where(key_mask[:, None, None, :], jnp.exp(scores - top_score[..., None]), 0.0)
    weight_sum = jnp.sum(weights, axis=-1)
    accumulated = jnp.einsum(
        "rhqk,rkhe->rhqe",
        weights.astype(jnp.bfloat16),
        value_heads,
        preferred_element_type=jnp.float32,
    )
    return (weight_sum, accumulated)


def body(video, text, patch_lengths, text_len, timestep, w_mod, w_qkv, w_out, stale_cache):
    section_index = lax.axis_index("section")
    seq_count = lax.axis_size("seq")
    requests, patches, per_dev, model_width = video.shape
    text_dev = text.shape[1]
    capacity = per_dev * seq_count
    text_slots = text_dev * seq_count
    column_count = w_out.shape[1]
    head_count = column_count // HEAD
    row_count = per_dev + text_dev
    modulated = lax.all_gather(modulation(timestep, w_mod[0]), "mp", axis=0, tiled=True)
    shift_vec = modulated[:model_width]
    scale_vec = modulated[model_width : 2 * model_width]
    gate_vec = modulated[2 * model_width :]
    weight_qkv = w_qkv[0].reshape(model_width, 3 * column_count)
    weight_out = w_out[0]
    stale_local = stale_cache[0]
    slot_index = jnp.arange(capacity, dtype=jnp.int32)
    video_valid = (slot_index[None, None, :] < patch_lengths[:, :, None]).reshape(requests, -1)
    text_valid = jnp.arange(text_slots, dtype=jnp.int32)[None, :] < text_len[:, None]
    all_valid = jnp.concatenate([video_valid, text_valid], axis=1)
    video_patch = jnp.repeat(jnp.arange(patches, dtype=jnp.int32), capacity)
    all_patch = jnp.concatenate([video_patch, jnp.zeros((text_slots,), jnp.int32)])
    stale_whole = lax.all_gather(stale_local, "seq", axis=2, tiled=True).reshape(
        requests, patches * capacity, 2, column_count
    )
    fresh_video = jnp.zeros((requests, patches, capacity, 2, column_count), jnp.bfloat16)
    fresh_text = jnp.zeros((requests, text_slots, 2, column_count), jnp.bfloat16)
    own_video = jnp.zeros((requests, patches, per_dev, 2, column_count), jnp.bfloat16)
    own_text = jnp.zeros((requests, text_dev, 2, column_count), jnp.bfloat16)
    out_video = jnp.zeros((requests, patches, per_dev, model_width), jnp.bfloat16)
    out_text = jnp.zeros((requests, text_dev, model_width), jnp.bfloat16)
    received = jnp.zeros((requests, row_count, model_width), jnp.bfloat16)
    patch_ids = jnp.arange(patches, dtype=jnp.int32)
    for turn_index in range(patches + 1):
        patch_now = turn_index - section_index
        picked = lax.dynamic_index_in_dim(
            video, jnp.clip(patch_now, 0, patches - 1), 1, keepdims=False
        )
        token_rows = jnp.where(
            section_index == 0, jnp.concatenate([picked, text], axis=1), received
        )
        normed = normalize(token_rows, shift_vec, scale_vec)
        projected = jnp.dot(
            normed.reshape(-1, model_width), weight_qkv, preferred_element_type=jnp.float32
        )
        projected = projected.reshape(requests, row_count, 3, column_count).astype(jnp.bfloat16)
        queries = projected[:, :, 0]
        key_value = projected[:, :, 1:]
        gathered_video, gathered_text = (
            lax.all_gather(key_value[:, :per_dev], "seq", axis=1, tiled=True),
            lax.all_gather(key_value[:, per_dev:], "seq", axis=1, tiled=True),
        )
        current = patch_ids == patch_now
        fresh_video = jnp.where(
            current[None, :, None, None, None], gathered_video[:, None], fresh_video
        )
        fresh_text = jnp.where(patch_now == 0, gathered_text, fresh_text)
        own_video = jnp.where(
            current[None, :, None, None, None], key_value[:, None, :per_dev], own_video
        )
        own_text = jnp.where(patch_now == 0, key_value[:, per_dev:], own_text)
        fresh_all = jnp.concatenate(
            [fresh_video.reshape(requests, patches * capacity, 2, column_count), fresh_text], axis=1
        )
        fresh_mask = all_valid & (all_patch[None, :] <= patch_now)
        query_heads = queries.reshape(requests, row_count, head_count, HEAD)
        scores, value_heads = scores_of(query_heads, fresh_all, head_count)
        fresh_top = masked_max(scores, fresh_mask)
        fresh_sum, fresh_acc = weighed(scores, fresh_mask, fresh_top, value_heads)
        stale_mask = video_valid & (video_patch[None, :] > patch_now)
        scores, value_heads = scores_of(query_heads, stale_whole, head_count)
        stale_top = masked_max(scores, stale_mask)
        stale_sum, stale_acc = weighed(scores, stale_mask, stale_top, value_heads)
        top_score = jnp.maximum(fresh_top, stale_top)
        fresh_weight = jnp.exp(fresh_top - top_score)
        stale_weight = jnp.exp(stale_top - top_score)
        numer = fresh_acc * fresh_weight[..., None] + stale_acc * stale_weight[..., None]
        denom = fresh_sum * fresh_weight + stale_sum * stale_weight
        attended = (numer / denom[..., None]).astype(jnp.bfloat16)
        attended = attended.transpose(0, 2, 1, 3).reshape(requests * row_count, column_count)
        partial_out = jnp.dot(attended, weight_out, preferred_element_type=jnp.float32).reshape(
            requests, row_count, model_width
        )
        summed = lax.psum(partial_out, "mp")
        result = (token_rows.astype(jnp.float32) + gate_vec * summed).astype(jnp.bfloat16)
        out_video = jnp.where(current[None, :, None, None], result[:, None, :per_dev], out_video)
        out_text = jnp.where(patch_now == 0, result[:, per_dev:], out_text)
        if turn_index < patches:
            received = passed_along(result, "section", 1)
    return (out_video[None], out_text[None], own_video[None], own_text[None])


def solution(mesh):
    placed = (
        P(None, None, "seq", None),
        P(None, "seq", None),
        P(),
        P(),
        P(),
        P("section", None, "mp"),
        P("section", None, None, "mp"),
        P("section", "mp", None),
        P("section", None, None, "seq", None, "mp"),
    )
    return jax.shard_map(
        body,
        mesh=mesh,
        in_specs=placed,
        out_specs=(
            P("section", None, None, "seq", None),
            P("section", None, "seq", None),
            P("section", None, None, "seq", None, "mp"),
            P("section", None, "seq", None, "mp"),
        ),
        check_vma=False,
    )
```

profile of v0, /device:TPU:0, one launch (start us, length us, event | category | flops | bytes accessed | tf_op | source)
XLA Modules:
  0.0 525.1 jit_solution(15506123433731643614)
XLA Ops:
  8.6 1.8 dynamic-slice_bitcast_fusion.4
  13.7 6.2 %all-gather.1 = f32[4,1,2304]{2,1,0:T(1,128)S(1)} all-gather(f32[1,1,2304]{2,1,0:T(1,128)S(1)} %convolution_bitcast_fusion), channel_id=1, replica_groups=mesh['section'=2,'seq'=4,'mp'=4] {'mp'}, dimensions={0}, use_global_device_ids=true | all-gather | bytes 46080 | tf_op jit(solution)/shard_map/all_gather | solution.py:73
  19.9 18.6 %copy.75 = bf16[1,3072,3,768]{1,3,2,0:T(8,128)(2,1)} copy(bf16[1,3072,3,768]{3,1,2,0:T(8,128)(2,1)} %param.15) | data formatting | bytes 28311552 | tf_op args[6]
  38.5 9.3 %fusion.21 = bf16[2,16,3,768]{3,1,2,0:T(8,128)(2,1)S(1)} fusion(bf16[1,3072,3,768]{1,3,2,0:T(8,128)(2,1)} %copy.75, f32[3072]{0:T(1024)S(1)} %get-tuple-element.76, f32[3072]{0:T(1024)S(1)} %get-tuple-element.77, f32[2,16]{1,0:T(2,128)S(1)} %add_rsqrt_fusion.4, f32[2,16]{1,0:T(2,128)S(1)} %broadcast_multiply_fusion.4, ...), kind=kOutput, calls=%fused_computation.27 | convolution fusion | flops 454139904 | bytes 14524673 | tf_op jit(solution)/shard_map/dot_general | solution.py:106
  47.9 14.4 %all_gather.37 = bf16[2,32,2,768]{3,1,2,0:T(8,128)(2,1)S(1)} all-gather(bf16[2,8,2,768]{3,1,2,0:T(8,128)(2,1)S(1)} %get-tuple-element.73), channel_id=1, replica_groups=mesh['section'=2,'seq'=4,'mp'=4] {'seq'}, dimensions={1}, use_global_device_ids=true | all-gather | bytes 245760 | tf_op jit(solution)/shard_map/all_gather | solution.py:113
  62.4 14.0 %all_gather.38 = bf16[2,32,2,768]{3,1,2,0:T(8,128)(2,1)S(1)} all-gather(bf16[2,8,2,768]{3,1,2,0:T(8,128)(2,1)S(1)} %get-tuple-element.74), channel_id=1, replica_groups=mesh['section'=2,'seq'=4,'mp'=4] {'seq'}, dimensions={1}, use_global_device_ids=true | all-gather | bytes 245760 | tf_op jit(solution)/shard_map/all_gather | solution.py:114
  78.9 17.7 %all-gather = bf16[1,2,4,32,2,768]{5,4,3,2,1,0:T(2,128)(2,1)S(1)} all-gather(bf16[1,2,4,8,2,768]{5,4,3,2,1,0:T(2,128)(2,1)S(1)} %copy-done.29), channel_id=2, replica_groups=mesh['section'=2,'seq'=4,'mp'=4] {'seq'}, dimensions={3}, use_global_device_ids=true | all-gather | bytes 983040 | tf_op jit(solution)/shard_map/all_gather | solution.py:86
  96.6 2.0 fusion.254
  98.6 2.2 copy.114
  102.1 1.8 copy.115
  110.1 1.4 fusion.56
  111.7 4.0 fusion.18
  115.8 34.1 %all-reduce.7.cloned.1.call-done = f32[2,16,3072]{2,1,0:T(8,128)} async-done(((f32[2,16,3072]{2,1,0:T(8,128)}), f32[2,16,3072]{2,1,0:T(8,128)}) %all-reduce.7.cloned.1.call-update) | async-done | bytes 393232 | tf_op jit(solution)/shard_map/psum | solution.py:147
  150.9 3.6 collective-permute-start
  154.7 2.8 collective-permute-done
  157.8 9.3 %fusion.24 = bf16[2,16,3,768]{3,1,2,0:T(8,128)(2,1)S(1)} fusion(bf16[1,3072,3,768]{1,3,2,0:T(8,128)(2,1)} %copy.75, bf16[2,16,3072]{2,1,0:T(8,128)(2,1)S(1)} %get-tuple-element.37, f32[2,16]{1,0:T(2,128)S(1)} %add_rsqrt_fusion.3, f32[2,16]{1,0:T(2,128)S(1)} %broadcast_multiply_fusion.3, f32[3072]{0:T(1024)S(1)} %get-tuple-element.76, ...), kind=kOutput, calls=%fused_computation.28 | convolution fusion | flops 453648384 | bytes 14524672 | tf_op jit(solution)/shard_map/dot_general | solution.py:106
  167.9 14.0 %all_gather.41 = bf16[2,32,2,768]{3,1,2,0:T(8,128)(2,1)S(1)} all-gather(bf16[2,8,2,768]{3,1,2,0:T(8,128)(2,1)S(1)} %get-tuple-element.72), channel_id=1, replica_groups=mesh['section'=2,'seq'=4,'mp'=4] {'seq'}, dimensions={1}, use_global_device_ids=true | all-gather | bytes 245760 | tf_op jit(solution)/shard_map/all_gather | solution.py:114
  181.9 13.7 %all_gather.40 = bf16[2,32,2,768]{3,1,2,0:T(8,128)(2,1)S(1)} all-gather(bf16[2,8,2,768]{3,1,2,0:T(8,128)(2,1)S(1)} %get-tuple-element.71), channel_id=1, replica_groups=mesh['section'=2,'seq'=4,'mp'=4] {'seq'}, dimensions={1}, use_global_device_ids=true | all-gather | bytes 245760 | tf_op jit(solution)/shard_map/all_gather | solution.py:113
  204.4 1.4 fusion.57
  206.0 4.0 fusion.16
  210.1 34.2 %all-reduce.9.cloned.1.call-done = f32[2,16,3072]{2,1,0:T(8,128)} async-done(((f32[2,16,3072]{2,1,0:T(8,128)}), f32[2,16,3072]{2,1,0:T(8,128)}) %all-reduce.9.cloned.1.call-update) | async-done | bytes 393232 | tf_op jit(solution)/shard_map/psum | solution.py:147
  245.3 3.4 collective-permute-start.1
  248.9 3.0 collective-permute-done.1
  252.2 9.3 %fusion.27 = bf16[2,16,3,768]{3,1,2,0:T(8,128)(2,1)S(1)} fusion(bf16[1,3072,3,768]{1,3,2,0:T(8,128)(2,1)} %copy.75, bf16[2,16,3072]{2,1,0:T(8,128)(2,1)S(1)} %get-tuple-element.32, f32[2,16]{1,0:T(2,128)S(1)} %add_rsqrt_fusion.2, f32[2,16]{1,0:T(2,128)S(1)} %broadcast_multiply_fusion.2, f32[3072]{0:T(1024)S(1)} %get-tuple-element.76, ...), kind=kOutput, calls=%fused_computation.29 | convolution fusion | flops 453648384 | bytes 14524672 | tf_op jit(solution)/shard_map/dot_general | solution.py:106
  261.7 14.0 %all_gather.43 = bf16[2,32,2,768]{3,1,2,0:T(8,128)(2,1)S(1)} all-gather(bf16[2,8,2,768]{3,1,2,0:T(8,128)(2,1)S(1)} %get-tuple-element.70), channel_id=1, replica_groups=mesh['section'=2,'seq'=4,'mp'=4] {'seq'}, dimensions={1}, use_global_device_ids=true | all-gather | bytes 245760 | tf_op jit(solution)/shard_map/all_gather | solution.py:114
  275.7 13.8 %all_gather.42 = bf16[2,32,2,768]{3,1,2,0:T(8,128)(2,1)S(1)} all-gather(bf16[2,8,2,768]{3,1,2,0:T(8,128)(2,1)S(1)} %get-tuple-element.69), channel_id=1, replica_groups=mesh['section'=2,'seq'=4,'mp'=4] {'seq'}, dimensions={1}, use_global_device_ids=true | all-gather | bytes 245760 | tf_op jit(solution)/shard_map/all_gather | solution.py:113
  295.7 1.4 fusion.58
  297.3 4.0 fusion.14
  301.4 34.3 %all-reduce.11.cloned.1.call-done = f32[2,16,3072]{2,1,0:T(8,128)} async-done(((f32[2,16,3072]{2,1,0:T(8,128)}), f32[2,16,3072]{2,1,0:T(8,128)}) %all-reduce.11.cloned.1.call-update) | async-done | bytes 393232 | tf_op jit(solution)/shard_map/psum | solution.py:147
  336.7 3.4 collective-permute-start.2
  340.3 3.0 collective-permute-done.2
  343.7 9.3 %fusion.30 = bf16[2,16,3,768]{3,1,2,0:T(8,128)(2,1)S(1)} fusion(bf16[1,3072,3,768]{1,3,2,0:T(8,128)(2,1)} %copy.75, bf16[2,16,3072]{2,1,0:T(8,128)(2,1)S(1)} %get-tuple-element.27, f32[2,16]{1,0:T(2,128)S(1)} %add_rsqrt_fusion.1, f32[2,16]{1,0:T(2,128)S(1)} %broadcast_multiply_fusion.1, f32[3072]{0:T(1024)S(1)} %get-tuple-element.76, ...), kind=kOutput, calls=%fused_computation.30 | convolution fusion | flops 453648384 | bytes 14524672 | tf_op jit(solution)/shard_map/dot_general | solution.py:106
  353.1 14.0 %all_gather.45 = bf16[2,32,2,768]{3,1,2,0:T(8,128)(2,1)S(1)} all-gather(bf16[2,8,2,768]{3,1,2,0:T(8,128)(2,1)S(1)} %get-tuple-element.68), channel_id=1, replica_groups=mesh['section'=2,'seq'=4,'mp'=4] {'seq'}, dimensions={1}, use_global_device_ids=true | all-gather | bytes 245760 | tf_op jit(solution)/shard_map/all_gather | solution.py:114
  367.1 13.7 %all_gather.44 = bf16[2,32,2,768]{3,1,2,0:T(8,128)(2,1)S(1)} all-gather(bf16[2,8,2,768]{3,1,2,0:T(8,128)(2,1)S(1)} %get-tuple-element.67), channel_id=1, replica_groups=mesh['section'=2,'seq'=4,'mp'=4] {'seq'}, dimensions={1}, use_global_device_ids=true | all-gather | bytes 245760 | tf_op jit(solution)/shard_map/all_gather | solution.py:113
  383.2 1.4 select_reduce_fusion.1
  385.6 1.4 fusion.59
  387.1 4.0 fusion.12
  391.2 34.2 %all-reduce.13.cloned.1.call-done = f32[2,16,3072]{2,1,0:T(8,128)} async-done(((f32[2,16,3072]{2,1,0:T(8,128)}), f32[2,16,3072]{2,1,0:T(8,128)}) %all-reduce.13.cloned.1.call-update) | async-done | bytes 393232 | tf_op jit(solution)/shard_map/psum | solution.py:147
  426.5 3.6 collective-permute-start.3
  433.4 9.3 %fusion.33 = bf16[2,16,3,768]{3,1,2,0:T(8,128)(2,1)S(1)} fusion(bf16[1,3072,3,768]{1,3,2,0:T(8,128)(2,1)} %copy.75, bf16[2,16,3072]{2,1,0:T(8,128)(2,1)S(1)} %get-tuple-element.22, f32[2,16]{1,0:T(2,128)S(1)} %add_rsqrt_fusion, f32[2,16]{1,0:T(2,128)S(1)} %broadcast_multiply_fusion, f32[3072]{0:T(1024)S(1)} %get-tuple-element.76, ...), kind=kOutput, calls=%fused_computation.31 | convolution fusion | flops 453648384 | bytes 14524672 | tf_op jit(solution)/shard_map/dot_general | solution.py:106
  442.8 1.6 select_bitcast_fusion
  445.0 13.6 %all_gather.46 = bf16[2,32,2,768]{3,1,2,0:T(8,128)(2,1)S(1)} all-gather(bf16[2,8,2,768]{3,1,2,0:T(8,128)(2,1)S(1)} %get-tuple-element.66), channel_id=1, replica_groups=mesh['section'=2,'seq'=4,'mp'=4] {'seq'}, dimensions={1}, use_global_device_ids=true | all-gather | bytes 245760 | tf_op jit(solution)/shard_map/all_gather | solution.py:113
  458.6 14.1 %all_gather.47 = bf16[2,32,2,768]{3,1,2,0:T(8,128)(2,1)S(1)} all-gather(bf16[2,8,2,768]{3,1,2,0:T(8,128)(2,1)S(1)} %get-tuple-element.65), channel_id=1, replica_groups=mesh['section'=2,'seq'=4,'mp'=4] {'seq'}, dimensions={1}, use_global_device_ids=true | all-gather | bytes 245760 | tf_op jit(solution)/shard_map/all_gather | solution.py:114
  475.2 1.4 fusion.60
  476.8 4.3 fusion.10
  481.1 1.5 copy.108
  482.6 1.9 broadcast_select_fusion.3
  484.5 30.9 %all-reduce.15.cloned.1.call-done = f32[2,16,3072]{2,1,0:T(8,128)} async-done(((f32[2,16,3072]{2,1,0:T(8,128)}), f32[2,16,3072]{2,1,0:T(8,128)}) %all-reduce.15.cloned.1.call-update) | async-done | bytes 393232 | tf_op jit(solution)/shard_map/psum | solution.py:147
  (268 shorter events, 48.6 us)
Async XLA Ops:
  7.2 142.7 %all-reduce.7.cloned.1.call-start = ((), (), s32[]{:S(2)}) async-start(), calls=%async_computation | async-start | bytes 786432 | tf_op jit(solution)/shard_map/psum | solution.py:147
  7.3 55.0 %copy-start.45 = (pred[4]{0:T(512)(128)(4,1)}, pred[4]{0:T(512)(128)(4,1)S(1)}, u32[]{:S(2)}) copy-start(pred[4]{0:T(512)(128)(4,1)S(1)} %iota_compare_fusion.4) | copy-start | bytes 16
  47.8 50.8 %copy-start.7 = (bf16[2,16,3,768]{3,1,2,0:T(8,128)(2,1)}, bf16[2,16,3,768]{3,1,2,0:T(8,128)(2,1)S(1)}, u32[]{:S(2)}) copy-start(bf16[2,16,3,768]{3,1,2,0:T(8,128)(2,1)S(1)} %fusion.21) | copy-start | bytes 442372
  47.8 29.9 %copy-start.55 = (s32[2,4]{1,0:T(2,128)S(1)}, s32[2,4]{1,0:T(2,128)}, u32[]{:S(2)}) copy-start(s32[2,4]{1,0:T(2,128)} %param.11) | copy-start | bytes 100
  47.8 30.2 %copy-start.56 = (s32[2]{0:T(128)S(1)}, s32[2]{0:T(128)}, u32[]{:S(2)}) copy-start(s32[2]{0:T(128)} %param.12) | copy-start | bytes 28
  47.8 31.0 %copy-start.29 = (bf16[1,2,4,8,2,768]{5,4,3,2,1,0:T(2,128)(2,1)S(1)}, bf16[1,2,4,8,2,768]{5,4,3,2,1,0:T(2,128)(2,1)}, u32[]{:S(2)}) copy-start(bf16[1,2,4,8,2,768]{5,4,3,2,1,0:T(2,128)(2,1)} %param.17) | copy-start | bytes 589828
  110.1 47.4 %copy-start.26 = (bf16[2,8,3072]{2,1,0:T(8,128)(2,1)S(1)}, bf16[2,8,3072]{2,1,0:T(8,128)(2,1)}, u32[]{:S(2)}) copy-start(bf16[2,8,3072]{2,1,0:T(8,128)(2,1)} %get-tuple-element.57) | copy-start | bytes 294916
  115.7 128.5 %all-reduce.9.cloned.1.call-start = ((), (), s32[]{:S(2)}) async-start(), calls=%async_computation.1 | async-start | bytes 786432 | tf_op jit(solution)/shard_map/psum | solution.py:147
  150.9 6.6 %collective-permute-start = (bf16[2,16,3072]{2,1,0:T(8,128)(2,1)S(1)}, bf16[2,16,3072]{2,1,0:T(8,128)(2,1)S(1)}, u32[]{:S(2)}, u32[]{:S(2)}) collective-permute-start(bf16[2,16,3072]{2,1,0:T(8,128)(2,1)S(1)} %fusion.96), channel_id=1, source_target_pairs={{0,16},{1,17},{2,18},{3,19},{4,20},{5,21},{6,22},{7,23},{8,24},{9,... | collective-permute-start | bytes 589832 | tf_op jit(solution)/shard_map/ppermute | solution.py:18
  154.7 40.9 %copy-start.34 = (pred[128]{0:T(512)(128)(4,1)}, pred[128]{0:T(512)(128)(4,1)S(1)}, u32[]{:S(2)}) copy-start(pred[128]{0:T(512)(128)(4,1)S(1)} %broadcast_in_dim.485) | copy-start | bytes 388
  157.8 37.8 %copy-start.31 = (pred[128]{0:T(512)(128)(4,1)S(1)}, pred[128]{0:T(512)(128)(4,1)}, u32[]{:S(2)}) copy-start(pred[128]{0:T(512)(128)(4,1)} %copy-done.30) | copy-start | bytes 388
  167.2 28.4 %copy-start.8 = (bf16[2,16,3,768]{3,1,2,0:T(8,128)(2,1)}, bf16[2,16,3,768]{3,1,2,0:T(8,128)(2,1)S(1)}, u32[]{:S(2)}) copy-start(bf16[2,16,3,768]{3,1,2,0:T(8,128)(2,1)S(1)} %fusion.24) | copy-start | bytes 442372
  167.2 33.2 %copy-start.39 = (pred[2,128]{1,0:T(4,128)(4,1)S(1)}, pred[2,128]{1,0:T(4,128)(4,1)}, u32[]{:S(2)}) copy-start(pred[2,128]{1,0:T(4,128)(4,1)} %get-tuple-element.90) | copy-start | bytes 772
  167.2 29.6 %copy-start.18 = (bf16[2,8,2,768]{3,1,2,0:T(8,128)(2,1)}, bf16[2,8,2,768]{3,1,2,0:T(8,128)(2,1)S(1)}, u32[]{:S(2)}) copy-start(bf16[2,8,2,768]{3,1,2,0:T(8,128)(2,1)S(1)} %get-tuple-element.71) | copy-start | bytes 147460
  210.0 125.7 %all-reduce.11.cloned.1.call-start = ((), (), s32[]{:S(2)}) async-start(), calls=%async_computation.2 | async-start | bytes 786432 | tf_op jit(solution)/shard_map/psum | solution.py:147
  245.3 6.6 %collective-permute-start.1 = (bf16[2,16,3072]{2,1,0:T(8,128)(2,1)S(1)}, bf16[2,16,3072]{2,1,0:T(8,128)(2,1)S(1)}, u32[]{:S(2)}, u32[]{:S(2)}) collective-permute-start(bf16[2,16,3072]{2,1,0:T(8,128)(2,1)S(1)} %fusion.97), channel_id=1, source_target_pairs={{0,16},{1,17},{2,18},{3,19},{4,20},{5,21},{6,22},{7,23},{8,24},{9,... | collective-permute-start | bytes 589832 | tf_op jit(solution)/shard_map/ppermute | solution.py:18
  248.9 40.6 %copy-start.42 = (pred[128]{0:T(512)(128)(4,1)}, pred[128]{0:T(512)(128)(4,1)S(1)}, u32[]{:S(2)}) copy-start(pred[128]{0:T(512)(128)(4,1)S(1)} %broadcast_in_dim.492) | copy-start | bytes 388
  252.2 37.3 %copy-start.4 = (bf16[2,32,2,768]{3,1,2,0:T(8,128)(2,1)S(1)}, bf16[2,32,2,768]{3,1,2,0:T(8,128)(2,1)}, u32[]{:S(2)}) copy-start(bf16[2,32,2,768]{3,1,2,0:T(8,128)(2,1)} %copy-done.3) | copy-start | bytes 589828
  252.2 37.3 %copy-start.32 = (pred[128]{0:T(512)(128)(4,1)S(1)}, pred[128]{0:T(512)(128)(4,1)}, u32[]{:S(2)}) copy-start(pred[128]{0:T(512)(128)(4,1)} %copy-done.30) | copy-start | bytes 388
  252.2 37.3 %copy-start.35 = (pred[128]{0:T(512)(128)(4,1)S(1)}, pred[128]{0:T(512)(128)(4,1)}, u32[]{:S(2)}) copy-start(pred[128]{0:T(512)(128)(4,1)} %copy-done.34) | copy-start | bytes 388
  261.6 27.9 %copy-start.9 = (bf16[2,16,3,768]{3,1,2,0:T(8,128)(2,1)}, bf16[2,16,3,768]{3,1,2,0:T(8,128)(2,1)S(1)}, u32[]{:S(2)}) copy-start(bf16[2,16,3,768]{3,1,2,0:T(8,128)(2,1)S(1)} %fusion.27) | copy-start | bytes 442372
  261.6 32.0 %copy-start.38 = (pred[2,128]{1,0:T(4,128)(4,1)S(1)}, pred[2,128]{1,0:T(4,128)(4,1)}, u32[]{:S(2)}) copy-start(pred[2,128]{1,0:T(4,128)(4,1)} %get-tuple-element.89) | copy-start | bytes 772
  261.6 27.8 %copy-start.20 = (bf16[2,8,2,768]{3,1,2,0:T(8,128)(2,1)}, bf16[2,8,2,768]{3,1,2,0:T(8,128)(2,1)S(1)}, u32[]{:S(2)}) copy-start(bf16[2,8,2,768]{3,1,2,0:T(8,128)(2,1)S(1)} %get-tuple-element.69) | copy-start | bytes 147460
  295.7 47.6 %copy-start.25 = (bf16[2,8,3072]{2,1,0:T(8,128)(2,1)S(1)}, bf16[2,8,3072]{2,1,0:T(8,128)(2,1)}, u32[]{:S(2)}) copy-start(bf16[2,8,3072]{2,1,0:T(8,128)(2,1)} %get-tuple-element.55) | copy-start | bytes 294916
  301.3 124.1 %all-reduce.13.cloned.1.call-start = ((), (), s32[]{:S(2)}) async-start(), calls=%async_computation.3 | async-start | bytes 786432 | tf_op jit(solution)/shard_map/psum | solution.py:147
  336.7 6.6 %collective-permute-start.2 = (bf16[2,16,3072]{2,1,0:T(8,128)(2,1)S(1)}, bf16[2,16,3072]{2,1,0:T(8,128)(2,1)S(1)}, u32[]{:S(2)}, u32[]{:S(2)}) collective-permute-start(bf16[2,16,3072]{2,1,0:T(8,128)(2,1)S(1)} %fusion.98), channel_id=1, source_target_pairs={{0,16},{1,17},{2,18},{3,19},{4,20},{5,21},{6,22},{7,23},{8,24},{9,... | collective-permute-start | bytes 589832 | tf_op jit(solution)/shard_map/ppermute | solution.py:18
  343.7 37.2 %copy-start.6 = (bf16[2,32,2,768]{3,1,2,0:T(8,128)(2,1)S(1)}, bf16[2,32,2,768]{3,1,2,0:T(8,128)(2,1)}, u32[]{:S(2)}) copy-start(bf16[2,32,2,768]{3,1,2,0:T(8,128)(2,1)} %copy-done.5) | copy-start | bytes 589828
  343.7 37.2 %copy-start.33 = (pred[128]{0:T(512)(128)(4,1)S(1)}, pred[128]{0:T(512)(128)(4,1)}, u32[]{:S(2)}) copy-start(pred[128]{0:T(512)(128)(4,1)} %copy-done.30) | copy-start | bytes 388
  343.7 37.2 %copy-start.36 = (pred[128]{0:T(512)(128)(4,1)S(1)}, pred[128]{0:T(512)(128)(4,1)}, u32[]{:S(2)}) copy-start(pred[128]{0:T(512)(128)(4,1)} %copy-done.34) | copy-start | bytes 388
  343.7 37.2 %copy-start.43 = (pred[128]{0:T(512)(128)(4,1)S(1)}, pred[128]{0:T(512)(128)(4,1)}, u32[]{:S(2)}) copy-start(pred[128]{0:T(512)(128)(4,1)} %copy-done.42) | copy-start | bytes 388
  353.1 27.8 %copy-start.10 = (bf16[2,16,3,768]{3,1,2,0:T(8,128)(2,1)}, bf16[2,16,3,768]{3,1,2,0:T(8,128)(2,1)S(1)}, u32[]{:S(2)}) copy-start(bf16[2,16,3,768]{3,1,2,0:T(8,128)(2,1)S(1)} %fusion.30) | copy-start | bytes 442372
  353.1 29.8 %copy-start.37 = (pred[2,128]{1,0:T(4,128)(4,1)S(1)}, pred[2,128]{1,0:T(4,128)(4,1)}, u32[]{:S(2)}) copy-start(pred[2,128]{1,0:T(4,128)(4,1)} %get-tuple-element.88) | copy-start | bytes 772
  353.1 27.8 %copy-start.22 = (bf16[2,8,2,768]{3,1,2,0:T(8,128)(2,1)}, bf16[2,8,2,768]{3,1,2,0:T(8,128)(2,1)S(1)}, u32[]{:S(2)}) copy-start(bf16[2,8,2,768]{3,1,2,0:T(8,128)(2,1)S(1)} %get-tuple-element.67) | copy-start | bytes 147460
  385.6 45.4 %copy-start.19 = (bf16[2,8,2,768]{3,1,2,0:T(8,128)(2,1)S(1)}, bf16[2,8,2,768]{3,1,2,0:T(8,128)(2,1)}, u32[]{:S(2)}) copy-start(bf16[2,8,2,768]{3,1,2,0:T(8,128)(2,1)} %copy-done.18) | copy-start | bytes 147460
  385.6 46.1 %copy-start.21 = (bf16[2,8,2,768]{3,1,2,0:T(8,128)(2,1)S(1)}, bf16[2,8,2,768]{3,1,2,0:T(8,128)(2,1)}, u32[]{:S(2)}) copy-start(bf16[2,8,2,768]{3,1,2,0:T(8,128)(2,1)} %copy-done.20) | copy-start | bytes 147460
  385.6 46.7 %copy-start.23 = (bf16[2,8,2,768]{3,1,2,0:T(8,128)(2,1)S(1)}, bf16[2,8,2,768]{3,1,2,0:T(8,128)(2,1)}, u32[]{:S(2)}) copy-start(bf16[2,8,2,768]{3,1,2,0:T(8,128)(2,1)} %copy-done.22) | copy-start | bytes 147460
  387.0 46.1 %copy-start.24 = (bf16[2,8,3072]{2,1,0:T(8,128)(2,1)S(1)}, bf16[2,8,3072]{2,1,0:T(8,128)(2,1)}, u32[]{:S(2)}) copy-start(bf16[2,8,3072]{2,1,0:T(8,128)(2,1)} %get-tuple-element.53) | copy-start | bytes 294916
  391.2 124.2 %all-reduce.15.cloned.1.call-start = ((), (), s32[]{:S(2)}) async-start(), calls=%async_computation.4 | async-start | bytes 786432 | tf_op jit(solution)/shard_map/psum | solution.py:147
  426.5 6.6 %collective-permute-start.3 = (bf16[2,16,3072]{2,1,0:T(8,128)(2,1)S(1)}, bf16[2,16,3072]{2,1,0:T(8,128)(2,1)S(1)}, u32[]{:S(2)}, u32[]{:S(2)}) collective-permute-start(bf16[2,16,3072]{2,1,0:T(8,128)(2,1)S(1)} %fusion.99), channel_id=1, source_target_pairs={{0,16},{1,17},{2,18},{3,19},{4,20},{5,21},{6,22},{7,23},{8,24},{9,... | collective-permute-start | bytes 589832 | tf_op jit(solution)/shard_map/ppermute | solution.py:18
  442.7 30.9 %copy-start.41 = (pred[2,128]{1,0:T(4,128)(4,1)S(1)}, pred[2,128]{1,0:T(4,128)(4,1)}, u32[]{:S(2)}) copy-start(pred[2,128]{1,0:T(4,128)(4,1)} %get-tuple-element.19) | copy-start | bytes 772
  476.6 39.9 %copy-start.12 = (bf16[2,16,3072]{2,1,0:T(8,128)(2,1)S(1)}, bf16[2,16,3072]{2,1,0:T(8,128)(2,1)}, u32[]{:S(2)}) copy-start(bf16[2,16,3072]{2,1,0:T(8,128)(2,1)} %copy-done.11) | copy-start | bytes 589828
  476.6 39.9 %copy-start.14 = (bf16[2,16,3072]{2,1,0:T(8,128)(2,1)S(1)}, bf16[2,16,3072]{2,1,0:T(8,128)(2,1)}, u32[]{:S(2)}) copy-start(bf16[2,16,3072]{2,1,0:T(8,128)(2,1)} %copy-done.13) | copy-start | bytes 589828
  476.6 39.9 %copy-start.16 = (bf16[2,16,3072]{2,1,0:T(8,128)(2,1)S(1)}, bf16[2,16,3072]{2,1,0:T(8,128)(2,1)}, u32[]{:S(2)}) copy-start(bf16[2,16,3072]{2,1,0:T(8,128)(2,1)} %copy-done.15) | copy-start | bytes 589828
  476.6 41.5 %copy-start.1 = (bf16[1,512,2304]{2,1,0:T(8,128)(2,1)S(1)}, bf16[1,512,2304]{2,1,0:T(8,128)(2,1)}, u32[]{:S(2)}) copy-start(bf16[1,512,2304]{2,1,0:T(8,128)(2,1)} %param.14) | copy-start | bytes 7077892
  476.8 40.4 %copy-start.48 = (pred[4]{0:T(512)(128)(4,1)S(1)}, pred[4]{0:T(512)(128)(4,1)}, u32[]{:S(2)}) copy-start(pred[4]{0:T(512)(128)(4,1)} %copy-done.47) | copy-start | bytes 16
  476.8 40.4 %copy-start.50 = (pred[4]{0:T(512)(128)(4,1)S(1)}, pred[4]{0:T(512)(128)(4,1)}, u32[]{:S(2)}) copy-start(pred[4]{0:T(512)(128)(4,1)} %copy-done.49) | copy-start | bytes 16
  476.8 40.4 %copy-start.52 = (pred[4]{0:T(512)(128)(4,1)S(1)}, pred[4]{0:T(512)(128)(4,1)}, u32[]{:S(2)}) copy-start(pred[4]{0:T(512)(128)(4,1)} %copy-done.51) | copy-start | bytes 16
  476.8 40.4 %copy-start.54 = (pred[4]{0:T(512)(128)(4,1)S(1)}, pred[4]{0:T(512)(128)(4,1)}, u32[]{:S(2)}) copy-start(pred[4]{0:T(512)(128)(4,1)} %copy-done.53) | copy-start | bytes 16
  (19 other events, 185.7 us)
Sparse Core Ops, SparseCore 0:
  115.9 33.9 all-reduce.6
  210.1 34.0 all-reduce.8
  301.4 34.2 all-reduce.10
  391.3 34.0 all-reduce.12
  481.2 34.1 all-reduce.14
where the time goes:
time: 534 us; the launch traced here: 525 us
  waiting for transfers between devices  177 us (33%)
  blocking collectives  163 us (31%)
  matrix products  83.4 us (16%)
  local copies, waits for them, and re-layouts  44.9 us (8%)
  other arithmetic  26.5 us (5%)
  between operations  16.1 us (3%)
  starting transfers between devices  14.2 us (3%)
    psum x5, waiting for transfers between devices, body(): summed = lax.psum(partial_out, 'mp')  168 us
    all_gather x5, blocking collectives, body(): lax.all_gather(key_value[:, per_dev:], 'seq', axis=1, tiled=True)  70.1 us
    all_gather x5, blocking collectives, body(): lax.all_gather(key_value[:, :per_dev], 'seq', axis=1, tiled=True)  69.2 us
    dot_general x5, matrix products, body(): jnp.dot(normed.reshape(-1, model_width), weight_qkv, preferred_element_ty...  46.6 us
    unnamed x118, local copies, waits for them, and re-layouts  24.4 us
    dot_general x5, matrix products, body(): jnp.dot(attended, weight_out, preferred_element_type=jnp.float32)  20.3 us
    all_gather x1, blocking collectives, body(): lax.all_gather(stale_local, 'seq', axis=2, tiled=True)  17.7 us
    ppermute x4, starting transfers between devices, passed_along(): lax.ppermute(value, axis, [(source, source + steps) for source in range(l...  14 us
  transfers between devices with their start and end apart: 9, of which 9 were waited for; matrix products, arithmetic and copies ran while one was open for 1% of the time, Pallas kernels for 0%

commit v1 on v0

v1 whole, which is shorter than its diff:
```python
import functools
import math

import jax
import jax.numpy as jnp
from jax import lax
from jax.experimental import pallas as pl
from jax.experimental.pallas import tpu as pltpu
from jax.sharding import PartitionSpec as P

HEAD = 64
EPS = 1e-05
NEG = -1e30
SLAB = 128
GROUP = 256
MESH = pl.DeviceIdType.MESH
F32 = jnp.float32
BF16 = jnp.bfloat16


def slot_marks(index, lengths_ref, text_ref, requests, first, patches, per_dev, text_dev, owner):
    req = jnp.zeros_like(index)
    patch = jnp.zeros_like(index)
    limit = jnp.zeros_like(index)
    start = jnp.zeros_like(index)
    at = 0
    for r in range(requests):
        for p in range(first, patches):
            inside = (index >= at) & (index < at + per_dev)
            req = jnp.where(inside, r, req)
            patch = jnp.where(inside, p, patch)
            limit = jnp.where(inside, lengths_ref[r, p], limit)
            start = jnp.where(inside, at, start)
            at += per_dev
    width = jnp.full_like(index, per_dev)
    for r in range(requests if text_dev else 0):
        inside = (index >= at) & (index < at + text_dev)
        req = jnp.where(inside, r, req)
        limit = jnp.where(inside, text_ref[r], limit)
        start = jnp.where(inside, at, start)
        width = jnp.where(inside, text_dev, width)
        at += text_dev
    live = owner * width + index - start < limit
    return req, patch, live


def split_index(shape, dim, size, count):
    index = lax.broadcasted_iota(jnp.int32, shape, dim)
    owner = jnp.zeros_like(index)
    for j in range(1, count):
        owner = owner + jnp.where(index >= j * size, 1, 0)
    return owner, index - owner * size


def kernel(dims, lengths_ref, text_len_ref, act_ref, video_ref, text_ref, stale_ref, w_mod_hbm,
           w_qkv_hbm, w_out_hbm, hidden_video, hidden_text, cache_video, cache_text,
           w_mod, w_qkv, w_out, x_buf, normed, query, attended, result, mod_all, kv_all, stale_all,
           part_send, part_recv, bias_f, bias_s,
           w_sem, mod_send, mod_recv, stale_send, stale_recv, kv_send, kv_recv, p_send, p_recv,
           x_cross_send, x_fwd_send, x_recv, res_send, res_recv):
    requests, patches, per_dev, text_dev, n_seq, n_mp, width, cols = dims
    rows = requests * (patches * per_dev + text_dev)
    video_rows = requests * patches * per_dev
    stale_rows = stale_ref.shape[1]
    groups = cols // GROUP
    section = lax.axis_index("section")
    seq = lax.axis_index("seq")
    mp = lax.axis_index("mp")
    other = 1 - section

    def at(sec, se, m):
        return (sec, se, m)

    weight_copies = [pltpu.make_async_copy(w_mod_hbm, w_mod, w_sem.at[0])]
    pieces = 3
    piece = width // pieces
    for part in (1, 2, 0):
        for i in range(pieces):
            weight_copies.append(pltpu.make_async_copy(
                w_qkv_hbm.at[part, pl.ds(i * piece, piece)],
                w_qkv.at[part, pl.ds(i * piece, piece)],
                w_sem.at[1 + part * pieces + i]))
    weight_copies.append(pltpu.make_async_copy(w_out_hbm, w_out, w_sem.at[1 + 3 * pieces]))
    for copy in weight_copies:
        copy.start()

    barrier = pltpu.get_barrier_semaphore()
    for k in range(1, n_mp):
        pl.semaphore_signal(barrier, inc=1, device_id=at(section, seq, lax.rem(mp + k, n_mp)), device_id_type=MESH)
    for k in range(1, n_seq):
        pl.semaphore_signal(barrier, inc=1, device_id=at(section, lax.rem(seq + k, n_seq), mp), device_id_type=MESH)
    pl.semaphore_signal(barrier, inc=1, device_id=at(other, seq, mp), device_id_type=MESH)

    weight_copies[0].wait()
    mod_all[mp] = jnp.dot(act_ref[...], w_mod[...], preferred_element_type=F32)
    stale_all[seq] = stale_ref[...]
    pl.semaphore_wait(barrier, n_mp - 1 + n_seq - 1 + 1)

    def mod_copy(k):
        return pltpu.make_async_remote_copy(
            src_ref=mod_all.at[mp], dst_ref=mod_all.at[mp], send_sem=mod_send.at[k],
            recv_sem=mod_recv.at[k], device_id=at(section, seq, lax.rem(mp + k, n_mp)), device_id_type=MESH)

    def mod_arrival(k):
        origin = lax.rem(mp + n_mp - k, n_mp)
        return pltpu.make_async_remote_copy(
            src_ref=mod_all.at[origin], dst_ref=mod_all.at[origin], send_sem=mod_send.at[k],
            recv_sem=mod_recv.at[k], device_id=at(section, seq, origin), device_id_type=MESH)

    def stale_copy(k, origin):
        return pltpu.make_async_remote_copy(
            src_ref=stale_all.at[origin], dst_ref=stale_all.at[origin], send_sem=stale_send.at[k],
            recv_sem=stale_recv.at[k], device_id=at(section, lax.rem(seq + k, n_seq), mp), device_id_type=MESH)

    for k in range(1, n_mp):
        mod_copy(k).start()
    for k in range(1, n_seq):
        stale_copy(k, seq).start()

    row_head, row_index = split_index((2 * rows, 1), 0, rows, 2)
    row_req, row_patch, _ = slot_marks(
        row_index, lengths_ref, text_len_ref, requests, 0, patches, per_dev, text_dev, row_head)
    key_owner, key_index = split_index((1, n_seq * rows), 1, rows, n_seq)
    key_req, key_patch, key_live = slot_marks(
        key_index, lengths_ref, text_len_ref, requests, 0, patches, per_dev, text_dev, key_owner)
    key_limit = jnp.where(key_live, key_patch, patches)
    bias_f[...] = jnp.where((row_req == key_req) & (key_limit <= row_patch), 0.0, NEG)
    key_owner, key_index = split_index((1, n_seq * stale_rows), 1, stale_rows, n_seq)
    key_req, key_patch, key_live = slot_marks(
        key_index, lengths_ref, text_len_ref, requests, 1, patches, per_dev, 0, key_owner)
    key_limit = jnp.where(key_live, key_patch, -1)
    bias_s[...] = jnp.where((row_req == key_req) & (key_limit > row_patch), 0.0, NEG)

    @pl.when(section == 0)
    def _():
        x_buf[pl.ds(0, video_rows)] = video_ref[...]
        x_buf[pl.ds(video_rows, rows - video_rows)] = text_ref[...]

    def block(j):
        return pl.ds(pl.multiple_of(j * cols, SLAB), cols)

    def cross_copy():
        return pltpu.make_async_remote_copy(
            src_ref=result.at[:, block(mp)], dst_ref=x_buf.at[:, block(mp)], send_sem=x_cross_send,
            recv_sem=x_recv.at[0], device_id=at(other, seq, mp), device_id_type=MESH)

    def forward_copy(k, origin):
        return pltpu.make_async_remote_copy(
            src_ref=x_buf.at[:, block(origin)], dst_ref=x_buf.at[:, block(origin)], send_sem=x_fwd_send.at[k],
            recv_sem=x_recv.at[k], device_id=at(section, seq, lax.rem(mp + k, n_mp)), device_id_type=MESH)

    for k in range(1, n_mp):
        mod_arrival(k).wait_recv()

    @pl.when(section == 1)
    def _():
        cross_copy().wait_recv()
        for k in range(1, n_mp):
            forward_copy(k, mp).start()
        for k in range(1, n_mp):
            forward_copy(k, lax.rem(mp + n_mp - k, n_mp)).wait_recv()

    def modulated(b):
        return mod_all[b // 3, 0:1, (b % 3) * cols:(b % 3 + 1) * cols]

    values = x_buf[...].astype(F32)
    mean = jnp.mean(values, axis=-1, keepdims=True)
    center = values - mean
    inverse = lax.rsqrt(jnp.mean(center * center, axis=-1, keepdims=True) + EPS)
    for c in range(n_mp):
        span = slice(c * cols, (c + 1) * cols)
        piece_values = (x_buf[:, span].astype(F32) - mean) * inverse
        normed[:, span] = (piece_values * (1.0 + modulated(n_mp + c)) + modulated(c)).astype(BF16)

    def kv_copy(g, k, origin):
        return pltpu.make_async_remote_copy(
            src_ref=kv_all.at[g, origin], dst_ref=kv_all.at[g, origin], send_sem=kv_send.at[g, k],
            recv_sem=kv_recv.at[g, k], device_id=at(section, lax.rem(seq + k, n_seq), mp), device_id_type=MESH)

    def project(part, g):
        return jnp.dot(normed[...], w_qkv[part, :, g * GROUP:(g + 1) * GROUP], preferred_element_type=F32)

    for copy in weight_copies[1:1 + pieces]:
        copy.wait()
    for g in range(groups):
        span = slice(g * GROUP, (g + 1) * GROUP)
        key = project(1, g).astype(BF16)
        if g == 0:
            for copy in weight_copies[1 + pieces:1 + 2 * pieces]:
                copy.wait()
        value = project(2, g).astype(BF16)
        kv_all[g, seq, :, 0:GROUP] = key
        kv_all[g, seq, :, GROUP:2 * GROUP] = value
        for k in range(1, n_seq):
            kv_copy(g, k, seq).start()
        cache_video[:, span] = key[:video_rows]
        cache_text[:, span] = key[video_rows:]
        span = slice(cols + g * GROUP, cols + (g + 1) * GROUP)
        cache_video[:, span] = value[:video_rows]
        cache_text[:, span] = value[video_rows:]
    for copy in weight_copies[1 + 2 * pieces:1 + 3 * pieces]:
        copy.wait()
    for g in range(groups):
        query[:, g * GROUP:(g + 1) * GROUP] = (project(0, g).astype(BF16).astype(F32) * HEAD ** (-0.5)).astype(BF16)

    for k in range(1, n_seq):
        stale_copy(k, lax.rem(seq + n_seq - k, n_seq)).wait_recv()
    low = lax.broadcasted_iota(jnp.int32, (rows, SLAB), 1) < HEAD
    contract_last = (((1,), (1,)), ((), ()))
    for g in range(groups):
        for k in range(1, n_seq):
            kv_copy(g, k, lax.rem(seq + n_seq - k, n_seq)).wait_recv()
        for h in range(GROUP // SLAB):
            span = slice(g * GROUP + h * SLAB, g * GROUP + (h + 1) * SLAB)
            k_span = slice(h * SLAB, (h + 1) * SLAB)
            v_span = slice(GROUP + h * SLAB, GROUP + (h + 1) * SLAB)
            slab = query[:, span]
            zero = jnp.zeros_like(slab)
            pair = jnp.concatenate([jnp.where(low, slab, zero), jnp.where(low, zero, slab)], axis=0)
            fresh_k = kv_all[g, :, :, k_span].reshape(n_seq * rows, SLAB)
            fresh_v = kv_all[g, :, :, v_span].reshape(n_seq * rows, SLAB)
            stale_k = stale_all[:, g, :, k_span].reshape(n_seq * stale_rows, SLAB)
            stale_v = stale_all[:, g, :, v_span].reshape(n_seq * stale_rows, SLAB)
            s_f = lax.dot_general(pair, fresh_k, contract_last, preferred_element_type=F32) + bias_f[...]
            s_s = lax.dot_general(pair, stale_k, contract_last, preferred_element_type=F32) + bias_s[...]
            top = jnp.maximum(jnp.max(s_f, axis=-1, keepdims=True), jnp.max(s_s, axis=-1, keepdims=True))
            e_f = jnp.exp(s_f - top)
            e_s = jnp.exp(s_s - top)
            total = jnp.sum(e_f, axis=-1, keepdims=True) + jnp.sum(e_s, axis=-1, keepdims=True)
            mixed = jnp.dot(e_f.astype(BF16), fresh_v, preferred_element_type=F32)
            mixed = mixed + jnp.dot(e_s.astype(BF16), stale_v, preferred_element_type=F32)
            mixed = mixed / total
            attended[:, span] = jnp.where(low, mixed[:rows], mixed[rows:]).astype(BF16)

    def part_copy(k):
        return pltpu.make_async_remote_copy(
            src_ref=part_send.at[k], dst_ref=part_recv.at[k], send_sem=p_send.at[k],
            recv_sem=p_recv.at[k], device_id=at(section, seq, lax.rem(mp + k, n_mp)), device_id_type=MESH)

    weight_copies[-1].wait()

    def out_block(j):
        return jnp.dot(attended[...], w_out[:, block(j)], preferred_element_type=F32)

    for k in range(1, n_mp):
        part_send[k] = out_block(lax.rem(mp + k, n_mp)).astype(BF16)
        part_copy(k).start()
    summed = out_block(mp)
    for k in range(1, n_mp):
        part_copy(k).wait_recv()
        summed = summed + part_recv[k].astype(F32)
    gate_at = 2 * n_mp + mp
    gate = mod_all[gate_at // 3, 0:1, pl.ds(pl.multiple_of(gate_at % 3 * cols, SLAB), cols)]
    result[:, block(mp)] = (x_buf[:, block(mp)].astype(F32) + gate * summed).astype(BF16)

    def result_copy(k, origin):
        return pltpu.make_async_remote_copy(
            src_ref=result.at[:, block(origin)], dst_ref=result.at[:, block(origin)], send_sem=res_send.at[k],
            recv_sem=res_recv.at[k], device_id=at(section, seq, lax.rem(mp + k, n_mp)), device_id_type=MESH)

    @pl.when(section == 0)
    def _():
        cross_copy().start()

    for k in range(1, n_mp):
        result_copy(k, mp).start()
    for k in range(1, n_mp):
        result_copy(k, lax.rem(mp + n_mp - k, n_mp)).wait_recv()
    hidden_video[...] = result[pl.ds(0, video_rows)]
    hidden_text[...] = result[pl.ds(video_rows, rows - video_rows)]

    @pl.when(section == 0)
    def _():
        cross_copy().wait_send()

    @pl.when(section == 1)
    def _():
        for k in range(1, n_mp):
            forward_copy(k, mp).wait_send()

    for k in range(1, n_mp):
        mod_copy(k).wait_send()
        part_copy(k).wait_send()
        result_copy(k, mp).wait_send()
    for k in range(1, n_seq):
        stale_copy(k, seq).wait_send()
        for g in range(groups):
            kv_copy(g, k, seq).wait_send()


def body(video, text, patch_lengths, text_len, timestep, w_mod, w_qkv, w_out, stale_cache):
    n_seq, n_mp = lax.axis_size("seq"), lax.axis_size("mp")
    requests, patches, per_dev, width = video.shape
    text_dev = text.shape[1]
    cols = w_out.shape[1]
    groups = cols // GROUP
    rows = requests * (patches * per_dev + text_dev)
    video_rows = requests * patches * per_dev
    text_rows = requests * text_dev
    stale_rows = requests * (patches - 1) * per_dev

    half_width = w_mod.shape[1] // 2
    frequency = jnp.exp(-math.log(10000.0) * jnp.arange(half_width, dtype=F32) / half_width)
    phases = timestep.astype(F32)[0] * frequency
    embedding = jnp.concatenate([jnp.cos(phases), jnp.sin(phases)])
    active = jax.nn.silu(embedding).astype(BF16)
    active = jnp.broadcast_to(active[None, :], (16, 2 * half_width))

    stale = stale_cache[0, :, 1:].reshape(stale_rows, 2, groups, GROUP)
    stale = stale.transpose(2, 0, 1, 3).reshape(groups, stale_rows, 2 * GROUP)

    mod_cols = w_mod.shape[2]
    dims = (requests, patches, per_dev, text_dev, n_seq, n_mp, width, cols)
    vmem = pl.BlockSpec(memory_space=pltpu.VMEM)
    smem = pl.BlockSpec(memory_space=pltpu.SMEM)
    hbm = pl.BlockSpec(memory_space=pl.ANY)
    dma = pltpu.SemaphoreType.DMA
    hidden_video, hidden_text, cache_video, cache_text = pl.pallas_call(
        functools.partial(kernel, dims),
        out_shape=(
            jax.ShapeDtypeStruct((video_rows, width), BF16),
            jax.ShapeDtypeStruct((text_rows, width), BF16),
            jax.ShapeDtypeStruct((video_rows, 2 * cols), BF16),
            jax.ShapeDtypeStruct((text_rows, 2 * cols), BF16),
        ),
        in_specs=[smem, smem, vmem, vmem, vmem, vmem, hbm, hbm, hbm],
        out_specs=(vmem,) * 4,
        scratch_shapes=[
            pltpu.VMEM(w_mod.shape[1:], BF16),
            pltpu.VMEM((3, width, cols), BF16),
            pltpu.VMEM((cols, width), BF16),
            pltpu.VMEM((rows, width), BF16),
            pltpu.VMEM((rows, width), BF16),
            pltpu.VMEM((rows, cols), BF16),
            pltpu.VMEM((rows, cols), BF16),
            pltpu.VMEM((rows, width), BF16),
            pltpu.VMEM((n_mp, 16, mod_cols), F32),
            pltpu.VMEM((groups, n_seq, rows, 2 * GROUP), BF16),
            pltpu.VMEM((n_seq, groups, stale_rows, 2 * GROUP), BF16),
            pltpu.VMEM((n_mp, rows, cols), BF16),
            pltpu.VMEM((n_mp, rows, cols), BF16),
            pltpu.VMEM((2 * rows, n_seq * rows), F32),
            pltpu.VMEM((2 * rows, n_seq * stale_rows), F32),
            dma((11,)),
            dma((n_mp,)), dma((n_mp,)),
            dma((n_seq,)), dma((n_seq,)),
            dma((groups, n_seq)), dma((groups, n_seq)),
            dma((n_mp,)), dma((n_mp,)),
            dma, dma((n_mp,)), dma((n_mp,)),
            dma((n_mp,)), dma((n_mp,)),
        ],
        compiler_params=pltpu.CompilerParams(
            collective_id=0, has_side_effects=True, vmem_limit_bytes=56 * 1024 * 1024
        ),
        cost_estimate=pl.CostEstimate(
            flops=2 * rows * width * 4 * cols, bytes_accessed=2 * width * (4 * cols + 2 * half_width), transcendentals=0
        ),
        name="layer",
    )(
        patch_lengths, text_len, active,
        video.reshape(video_rows, width), text.reshape(text_rows, width), stale,
        w_mod[0], w_qkv[0].transpose(1, 0, 2), w_out[0],
    )
    return (
        hidden_video.reshape(1, requests, patches, per_dev, width),
        hidden_text.reshape(1, requests, text_dev, width),
        cache_video.reshape(1, requests, patches, per_dev, 2, cols),
        cache_text.reshape(1, requests, text_dev, 2, cols),
    )


def solution(mesh):
    placed = (
        P(None, None, "seq", None),
        P(None, "seq", None),
        P(),
        P(),
        P(),
        P("section", None, "mp"),
        P("section", None, None, "mp"),
        P("section", "mp", None),
        P("section", None, None, "seq", None, "mp"),
    )
    return jax.shard_map(
        body,
        mesh=mesh,
        in_specs=placed,
        out_specs=(
            P("section", None, None, "seq", None),
            P("section", None, "seq", None),
            P("section", None, None, "seq", None, "mp"),
            P("section", None, "seq", None, "mp"),
        ),
        check_vma=False,
    )
```

time: 534 us -> 106 us (0.20)
  the two profiles are of different devices: /device:TPU:0 before, /device:TPU:3 now
where the time goes in v1:
time: 106 us; the launch traced here: 104 us
  Pallas kernels  93.8 us (88%)
  local copies, waits for them, and re-layouts  9.17 us (9%)
  between operations  1.32 us (1%)
    pallas_call x1, Pallas kernels, body(): pl.pallas_call(functools.partial(kernel, dims), out_shape=(jax.ShapeDtype...  93.8 us
    unnamed x4, local copies, waits for them, and re-layouts  6.52 us

profile of v1, /device:TPU:3, one launch (start us, length us, event | category | flops | bytes accessed | tf_op | source)
XLA Modules:
  0.0 104.4 jit_solution(10391061526012521714)
XLA Ops:
  1.4 0.6 broadcast_in_dim.2.act_ref
  2.0 1.0 slice.3
  3.0 0.1 reshape_squeeze.3
  3.1 0.2 copy.17
  3.3 0.8 reshape.57.stale_ref
  4.0 93.8 %layer.1 = (bf16[64,3072]{1,0:T(8,128)(2,1)}, bf16[16,3072]{1,0:T(8,128)(2,1)}, bf16[64,1536]{1,0:T(8,128)(2,1)}, bf16[16,1536]{1,0:T(8,128)(2,1)}) custom-call(s32[2,4]{1,0:T(2,128)} %lengths_ref.1, s32[2]{0:T(128)} %text_len_ref.1, bf16[16,512]{1,0:T(8,128)(2,1)} %broadcast_in_dim.2.act_ref, bf16[64,3072]{1,0:T(8,128)(2,1)} %bitcast.22, ...), custom_call_target="tpu_custom_call" | custom-call | flops 1509949440 | bytes 22020096 | tf_op jit(solution)/shard_map/layer/pallas_call | solution.py:318
  97.8 1.5 %copy.19 = bf16[1,2,8,2,768]{4,3,2,1,0:T(2,128)(2,1)} copy(bf16[1,2,8,2,768]{4,2,3,1,0:T(8,128)(2,1)} %bitcast.26) | data formatting | bytes 98304
  99.3 1.8 %copy.18 = bf16[1,2,4,8,2,768]{5,4,3,2,1,0:T(2,128)(2,1)} copy(bf16[1,2,4,8,2,768]{5,3,4,2,1,0:T(8,128)(2,1)} %bitcast.23) | data formatting | bytes 393216
  101.1 1.8 %copy.23 = bf16[1,2,4,8,3072]{4,3,2,1,0:T(8,128)(2,1)} copy(bf16[1,2,4,8,3072]{4,3,2,1,0:T(8,128)(2,1)} %bitcast.21) | data formatting | bytes 786432
  102.8 1.5 %copy.24 = bf16[1,2,8,3072]{3,2,1,0:T(8,128)(2,1)} copy(bf16[1,2,8,3072]{3,2,1,0:T(8,128)(2,1)} %bitcast.25) | data formatting | bytes 196608
  (3 shorter events, 0.1 us)

commit v2 on v1

--- a/solution.py
+++ b/solution.py
@@ -57,16 +57,21 @@
            w_mod, w_qkv, w_out, x_buf, normed, query, attended, result, mod_all, kv_all, stale_all,
            part_send, part_recv, bias_f, bias_s,
            w_sem, mod_send, mod_recv, stale_send, stale_recv, kv_send, kv_recv, p_send, p_recv,
-           x_cross_send, x_fwd_send, x_recv, res_send, res_recv):
+           cross_send, cross_recv, x_send, x_recv, res_send, res_recv):
     requests, patches, per_dev, text_dev, n_seq, n_mp, width, cols = dims
     rows = requests * (patches * per_dev + text_dev)
     video_rows = requests * patches * per_dev
-    stale_rows = stale_ref.shape[1]
+    stale_rows = requests * (patches - 1) * per_dev
     groups = cols // GROUP
     section = lax.axis_index("section")
     seq = lax.axis_index("seq")
     mp = lax.axis_index("mp")
     other = 1 - section
+    core_mate = mp + 1 - 2 * lax.rem(mp, 2)
+    y_mate = lax.rem(mp + 2, n_mp)
+    diagonal = lax.rem(core_mate + 2, n_mp)
+    half = rows // 32 * 16 + 16 * (rows // 16 % 2)
+    row_pieces = (pl.ds(0, half), pl.ds(half, rows - half))
 
     def at(sec, se, m):
         return (sec, se, m)
@@ -92,8 +97,15 @@
     pl.semaphore_signal(barrier, inc=1, device_id=at(other, seq, mp), device_id_type=MESH)
 
     weight_copies[0].wait()
-    mod_all[mp] = jnp.dot(act_ref[...], w_mod[...], preferred_element_type=F32)
-    stale_all[seq] = stale_ref[...]
+    active = jnp.broadcast_to(act_ref[...].astype(F32), (8, act_ref.shape[1])).astype(BF16)
+    mod_all[mp] = jnp.dot(active, w_mod[...], preferred_element_type=F32)
+    span_all = patches * per_dev
+    for kind in range(2):
+        whole = stale_ref[:, kind, :].astype(F32)
+        kept = jnp.concatenate(
+            [whole[r * span_all + per_dev:(r + 1) * span_all] for r in range(requests)], axis=0).astype(BF16)
+        for g in range(groups):
+            stale_all[seq, g, :, kind * GROUP:(kind + 1) * GROUP] = kept[:, g * GROUP:(g + 1) * GROUP]
     pl.semaphore_wait(barrier, n_mp - 1 + n_seq - 1 + 1)
 
     def mod_copy(k):
@@ -139,26 +151,45 @@
     def block(j):
         return pl.ds(pl.multiple_of(j * cols, SLAB), cols)
 
-    def cross_copy():
-        return pltpu.make_async_remote_copy(
-            src_ref=result.at[:, block(mp)], dst_ref=x_buf.at[:, block(mp)], send_sem=x_cross_send,
-            recv_sem=x_recv.at[0], device_id=at(other, seq, mp), device_id_type=MESH)
-
-    def forward_copy(k, origin):
-        return pltpu.make_async_remote_copy(
-            src_ref=x_buf.at[:, block(origin)], dst_ref=x_buf.at[:, block(origin)], send_sem=x_fwd_send.at[k],
-            recv_sem=x_recv.at[k], device_id=at(section, seq, lax.rem(mp + k, n_mp)), device_id_type=MESH)
+    def cross_copy(c):
+        return pltpu.make_async_remote_copy(
+            src_ref=result.at[row_pieces[c], block(mp)], dst_ref=x_buf.at[row_pieces[c], block(mp)],
+            send_sem=cross_send.at[c], recv_sem=cross_recv.at[c], device_id=at(other, seq, mp), device_id_type=MESH)
+
+    def spread_copy(buffer, sems, c, kind, origin):
+        part = buffer.at[row_pieces[c], block(origin)]
+        return pltpu.make_async_remote_copy(
+            src_ref=part, dst_ref=part, send_sem=sems[0].at[c, kind], recv_sem=sems[1].at[c, kind],
+            device_id=at(section, seq, y_mate if kind == 1 else core_mate), device_id_type=MESH)
+
+    def spread_start(buffer, sems, c):
+        spread_copy(buffer, sems, c, 1, mp).start()
+        spread_copy(buffer, sems, c, 0, mp).start()
+
+    def spread_finish(buffer, sems):
+        for c in range(2):
+            spread_copy(buffer, sems, c, 1, y_mate).wait_recv()
+            spread_copy(buffer, sems, c, 2, y_mate).start()
+        for c in range(2):
+            spread_copy(buffer, sems, c, 0, core_mate).wait_recv()
+            spread_copy(buffer, sems, c, 2, diagonal).wait_recv()
+
+    def spread_sent(buffer, sems):
+        for c in range(2):
+            for kind, origin in enumerate((mp, mp, y_mate)):
+                spread_copy(buffer, sems, c, kind, origin).wait_send()
+
+    x_sems, result_sems = (x_send, x_recv), (res_send, res_recv)
 
     for k in range(1, n_mp):
         mod_arrival(k).wait_recv()
 
     @pl.when(section == 1)
     def _():
-        cross_copy().wait_recv()
-        for k in range(1, n_mp):
-            forward_copy(k, mp).start()
-        for k in range(1, n_mp):
-            forward_copy(k, lax.rem(mp + n_mp - k, n_mp)).wait_recv()
+        for c in range(2):
+            cross_copy(c).wait_recv()
+            spread_start(x_buf, x_sems, c)
+        spread_finish(x_buf, x_sems)
 
     def modulated(b):
         return mod_all[b // 3, 0:1, (b % 3) * cols:(b % 3 + 1) * cols]
@@ -183,7 +214,6 @@
     for copy in weight_copies[1:1 + pieces]:
         copy.wait()
     for g in range(groups):
-        span = slice(g * GROUP, (g + 1) * GROUP)
         key = project(1, g).astype(BF16)
         if g == 0:
             for copy in weight_copies[1 + pieces:1 + 2 * pieces]:
@@ -193,15 +223,17 @@
         kv_all[g, seq, :, GROUP:2 * GROUP] = value
         for k in range(1, n_seq):
             kv_copy(g, k, seq).start()
-        cache_video[:, span] = key[:video_rows]
-        cache_text[:, span] = key[video_rows:]
-        span = slice(cols + g * GROUP, cols + (g + 1) * GROUP)
-        cache_video[:, span] = value[:video_rows]
-        cache_text[:, span] = value[video_rows:]
     for copy in weight_copies[1 + 2 * pieces:1 + 3 * pieces]:
         copy.wait()
     for g in range(groups):
         query[:, g * GROUP:(g + 1) * GROUP] = (project(0, g).astype(BF16).astype(F32) * HEAD ** (-0.5)).astype(BF16)
+
+    for g in range(groups):
+        for kind in range(2):
+            span = slice(g * GROUP, (g + 1) * GROUP)
+            part = kv_all[g, seq, :, kind * GROUP:(kind + 1) * GROUP]
+            cache_video[:, kind, span] = part[:video_rows]
+            cache_text[:, kind, span] = part[video_rows:]
 
     for k in range(1, n_seq):
         stale_copy(k, lax.rem(seq + n_seq - k, n_seq)).wait_recv()
@@ -234,58 +266,69 @@
 
     def part_copy(k):
         return pltpu.make_async_remote_copy(
-            src_ref=part_send.at[k], dst_ref=part_recv.at[k], send_sem=p_send.at[k],
-            recv_sem=p_recv.at[k], device_id=at(section, seq, lax.rem(mp + k, n_mp)), device_id_type=MESH)
+            src_ref=part_send.at[k], dst_ref=part_recv.at[k], send_sem=p_send.at[k], recv_sem=p_recv.at[k],
+            device_id=at(section, seq, y_mate if k == 2 else core_mate), device_id_type=MESH)
 
     weight_copies[-1].wait()
 
     def out_block(j):
         return jnp.dot(attended[...], w_out[:, block(j)], preferred_element_type=F32)
 
-    for k in range(1, n_mp):
-        part_send[k] = out_block(lax.rem(mp + k, n_mp)).astype(BF16)
-        part_copy(k).start()
+    part_send[0] = out_block(diagonal).astype(BF16)
+    part_copy(0).start()
+    passed = out_block(y_mate)
+    part_copy(0).wait_recv()
+    part_send[2] = (passed + part_recv[0].astype(F32)).astype(BF16)
+    part_copy(2).start()
+    part_send[1] = out_block(core_mate).astype(BF16)
+    part_copy(1).start()
     summed = out_block(mp)
-    for k in range(1, n_mp):
-        part_copy(k).wait_recv()
-        summed = summed + part_recv[k].astype(F32)
+    part_copy(1).wait_recv()
+    summed = summed + part_recv[1].astype(F32)
+    part_copy(2).wait_recv()
+    summed = summed + part_recv[2].astype(F32)
     gate_at = 2 * n_mp + mp
     gate = mod_all[gate_at // 3, 0:1, pl.ds(pl.multiple_of(gate_at % 3 * cols, SLAB), cols)]
     result[:, block(mp)] = (x_buf[:, block(mp)].astype(F32) + gate * summed).astype(BF16)
 
-    def result_copy(k, origin):
-        return pltpu.make_async_remote_copy(
-            src_ref=result.at[:, block(origin)], dst_ref=result.at[:, block(origin)], send_sem=res_send.at[k],
-            recv_sem=res_recv.at[k], device_id=at(section, seq, lax.rem(mp + k, n_mp)), device_id_type=MESH)
-
     @pl.when(section == 0)
     def _():
-        cross_copy().start()
-
-    for k in range(1, n_mp):
-        result_copy(k, mp).start()
-    for k in range(1, n_mp):
-        result_copy(k, lax.rem(mp + n_mp - k, n_mp)).wait_recv()
+        for c in range(2):
+            cross_copy(c).start()
+
+    for c in range(2):
+        spread_start(result, result_sems, c)
+    spread_finish(result, result_sems)
     hidden_video[...] = result[pl.ds(0, video_rows)]
     hidden_text[...] = result[pl.ds(video_rows, rows - video_rows)]
 
     @pl.when(section == 0)
     def _():
-        cross_copy().wait_send()
+        for c in range(2):
+            cross_copy(c).wait_send()
 
     @pl.when(section == 1)
     def _():
-        for k in range(1, n_mp):
-            forward_copy(k, mp).wait_send()
-
+        spread_sent(x_buf, x_sems)
+
+    spread_sent(result, result_sems)
     for k in range(1, n_mp):
         mod_copy(k).wait_send()
+    for k in range(3):
         part_copy(k).wait_send()
-        result_copy(k, mp).wait_send()
     for k in range(1, n_seq):
         stale_copy(k, seq).wait_send()
         for g in range(groups):
             kv_copy(g, k, seq).wait_send()
+
+
+def store_kernel(*refs):
+    sems = refs[-1]
+    copies = [pltpu.make_async_copy(refs[i], refs[4 + i], sems.at[i]) for i in range(4)]
+    for copy in copies:
+        copy.start()
+    for copy in copies:
+        copy.wait()
 
 
 def body(video, text, patch_lengths, text_len, timestep, w_mod, w_qkv, w_out, stale_cache):
@@ -304,10 +347,6 @@
     phases = timestep.astype(F32)[0] * frequency
     embedding = jnp.concatenate([jnp.cos(phases), jnp.sin(phases)])
     active = jax.nn.silu(embedding).astype(BF16)
-    active = jnp.broadcast_to(active[None, :], (16, 2 * half_width))
-
-    stale = stale_cache[0, :, 1:].reshape(stale_rows, 2, groups, GROUP)
-    stale = stale.transpose(2, 0, 1, 3).reshape(groups, stale_rows, 2 * GROUP)
 
     mod_cols = w_mod.shape[2]
     dims = (requests, patches, per_dev, text_dev, n_seq, n_mp, width, cols)
@@ -315,13 +354,13 @@
     smem = pl.BlockSpec(memory_space=pltpu.SMEM)
     hbm = pl.BlockSpec(memory_space=pl.ANY)
     dma = pltpu.SemaphoreType.DMA
-    hidden_video, hidden_text, cache_video, cache_text = pl.pallas_call(
+    outputs = pl.pallas_call(
         functools.partial(kernel, dims),
         out_shape=(
             jax.ShapeDtypeStruct((video_rows, width), BF16),
             jax.ShapeDtypeStruct((text_rows, width), BF16),
-            jax.ShapeDtypeStruct((video_rows, 2 * cols), BF16),
-            jax.ShapeDtypeStruct((text_rows, 2 * cols), BF16),
+            jax.ShapeDtypeStruct((video_rows, 2, cols), BF16),
+            jax.ShapeDtypeStruct((text_rows, 2, cols), BF16),
         ),
         in_specs=[smem, smem, vmem, vmem, vmem, vmem, hbm, hbm, hbm],
         out_specs=(vmem,) * 4,
@@ -334,11 +373,11 @@
             pltpu.VMEM((rows, cols), BF16),
             pltpu.VMEM((rows, cols), BF16),
             pltpu.VMEM((rows, width), BF16),
-            pltpu.VMEM((n_mp, 16, mod_cols), F32),
+            pltpu.VMEM((n_mp, 8, mod_cols), F32),
             pltpu.VMEM((groups, n_seq, rows, 2 * GROUP), BF16),
             pltpu.VMEM((n_seq, groups, stale_rows, 2 * GROUP), BF16),
-            pltpu.VMEM((n_mp, rows, cols), BF16),
-            pltpu.VMEM((n_mp, rows, cols), BF16),
+            pltpu.VMEM((3, rows, cols), BF16),
+            pltpu.VMEM((3, rows, cols), BF16),
             pltpu.VMEM((2 * rows, n_seq * rows), F32),
             pltpu.VMEM((2 * rows, n_seq * stale_rows), F32),
             dma((11,)),
@@ -346,8 +385,9 @@
             dma((n_seq,)), dma((n_seq,)),
             dma((groups, n_seq)), dma((groups, n_seq)),
             dma((n_mp,)), dma((n_mp,)),
-            dma, dma((n_mp,)), dma((n_mp,)),
-            dma((n_mp,)), dma((n_mp,)),
+            dma((2,)), dma((2,)),
+            dma((2, 3)), dma((2, 3)),
+            dma((2, 3)), dma((2, 3)),
         ],
         compiler_params=pltpu.CompilerParams(
             collective_id=0, has_side_effects=True, vmem_limit_bytes=56 * 1024 * 1024
@@ -357,10 +397,19 @@
         ),
         name="layer",
     )(
-        patch_lengths, text_len, active,
-        video.reshape(video_rows, width), text.reshape(text_rows, width), stale,
+        patch_lengths, text_len, active[None, :],
+        video.reshape(video_rows, width), text.reshape(text_rows, width), stale_cache.reshape(video_rows, 2, cols),
         w_mod[0], w_qkv[0].transpose(1, 0, 2), w_out[0],
     )
+    hidden_video, hidden_text, cache_video, cache_text = pl.pallas_call(
+        store_kernel,
+        out_shape=tuple(jax.ShapeDtypeStruct(o.shape, o.dtype) for o in outputs),
+        in_specs=[hbm] * 4,
+        out_specs=(hbm,) * 4,
+        scratch_shapes=[dma((4,))],
+        compiler_params=pltpu.CompilerParams(vmem_limit_bytes=56 * 1024 * 1024),
+        name="store",
+    )(*outputs)
     return (
         hidden_video.reshape(1, requests, patches, per_dev, width),
         hidden_text.reshape(1, requests, text_dev, width),

time: 106 us -> 118 us (1.11)
  Pallas kernels: 93.8 us -> 114 us
  local copies, waits for them, and re-layouts: 9.17 us -> 0 us
    pallas_call x0 -> x1, Pallas kernels: none -> 23.5 us  [body(): pl.pallas_call(store_kernel, out_shape=tuple((jax.ShapeDtypeStruct(o.shap...]
    unnamed x4 -> x0, local copies, waits for them, and re-layouts: 6.52 us -> none
    pallas_call x1, Pallas kernels: 93.8 us -> 90.8 us  [body(): pl.pallas_call(functools.partial(kernel, dims), out_shape=(jax.ShapeDtype...]
where the time goes in v2:
time: 118 us; the launch traced here: 116 us
  Pallas kernels  114 us (97%)
  between operations  1.29 us (1%)
    pallas_call x1, Pallas kernels, body(): pl.pallas_call(functools.partial(kernel, dims), out_shape=(jax.ShapeDtype...  90.8 us
    pallas_call x1, Pallas kernels, body(): pl.pallas_call(store_kernel, out_shape=tuple((jax.ShapeDtypeStruct(o.shap...  23.5 us

profile of v2, /device:TPU:3, one launch (start us, length us, event | category | flops | bytes accessed | tf_op | source)
XLA Modules:
  0.0 116.2 jit_solution(8704646951750662672)
XLA Ops:
  1.3 0.6 fusion.act_ref
  1.9 90.8 %layer.1 = (bf16[64,3072]{1,0:T(8,128)(2,1)}, bf16[16,3072]{1,0:T(8,128)(2,1)}, bf16[64,2,768]{2,1,0:T(2,128)(2,1)}, bf16[16,2,768]{2,1,0:T(2,128)(2,1)}) custom-call(s32[2,4]{1,0:T(2,128)} %lengths_ref.1, s32[2]{0:T(128)} %text_len_ref.1, bf16[1,512]{1,0:T(2,128)(2,1)} %fusion.act_ref, bf16[64,3072]{1,0:T(8,128)(2,1)} %bitcast.18, ...), custom_call_target="tpu_custom_call" | custom-call | flops 1509949440 | bytes 22020096 | tf_op jit(solution)/shard_map/layer/pallas_call | solution.py:357
  92.7 23.5 %store.1 = (bf16[64,3072]{1,0:T(8,128)(2,1)}, bf16[16,3072]{1,0:T(8,128)(2,1)}, bf16[64,2,768]{2,1,0:T(2,128)(2,1)}, bf16[16,2,768]{2,1,0:T(2,128)(2,1)}) custom-call(bf16[64,3072]{1,0:T(8,128)(2,1)} %get-tuple-element.12.refs_0_, bf16[16,3072]{1,0:T(8,128)(2,1)} %get-tuple-element.13.refs_1_, bf16[64,2,768]{2,1,0:T(2,128)(2,1)} %get-tuple-element.14.refs_2_, ...), custom_call_target="tpu_custom_call" | custom-call | tf_op jit(solution)/shard_map/store/pallas_call | solution.py:404
  (1 shorter events, 0.0 us)

commit v3 on v2

--- a/solution.py
+++ b/solution.py
@@ -54,15 +54,18 @@
 
 def kernel(dims, lengths_ref, text_len_ref, act_ref, video_ref, text_ref, stale_ref, w_mod_hbm,
            w_qkv_hbm, w_out_hbm, hidden_video, hidden_text, cache_video, cache_text,
-           w_mod, w_qkv, w_out, x_buf, normed, query, attended, result, mod_all, kv_all, stale_all,
-           part_send, part_recv, bias_f, bias_s,
-           w_sem, mod_send, mod_recv, stale_send, stale_recv, kv_send, kv_recv, p_send, p_recv,
+           w_mod, w_qkv, w_out, x_buf, normed, projected, attended, result, mod_all, heads_send, heads_recv,
+           back_send, back_recv, stale_send_buf, stale_recv_buf, key_cat, value_cat, part_send, part_recv, bias,
+           w_sem, mod_send, mod_recv, stale_send, stale_recv, heads_out, heads_in, back_out, back_in, p_send, p_recv,
            cross_send, cross_recv, x_send, x_recv, res_send, res_recv):
     requests, patches, per_dev, text_dev, n_seq, n_mp, width, cols = dims
     rows = requests * (patches * per_dev + text_dev)
     video_rows = requests * patches * per_dev
     stale_rows = requests * (patches - 1) * per_dev
     groups = cols // GROUP
+    each, active = head_split(cols // HEAD, n_seq)
+    share = each * HEAD
+    fresh_keys = n_seq * rows
     section = lax.axis_index("section")
     seq = lax.axis_index("seq")
     mp = lax.axis_index("mp")
@@ -97,15 +100,15 @@
     pl.semaphore_signal(barrier, inc=1, device_id=at(other, seq, mp), device_id_type=MESH)
 
     weight_copies[0].wait()
-    active = jnp.broadcast_to(act_ref[...].astype(F32), (8, act_ref.shape[1])).astype(BF16)
-    mod_all[mp] = jnp.dot(active, w_mod[...], preferred_element_type=F32)
+    act = jnp.broadcast_to(act_ref[...].astype(F32), (8, act_ref.shape[1])).astype(BF16)
+    mod_all[mp] = jnp.dot(act, w_mod[...], preferred_element_type=F32)
     span_all = patches * per_dev
     for kind in range(2):
         whole = stale_ref[:, kind, :].astype(F32)
         kept = jnp.concatenate(
             [whole[r * span_all + per_dev:(r + 1) * span_all] for r in range(requests)], axis=0).astype(BF16)
-        for g in range(groups):
-            stale_all[seq, g, :, kind * GROUP:(kind + 1) * GROUP] = kept[:, g * GROUP:(g + 1) * GROUP]
+        for d in range(active):
+            stale_send_buf[d, :, kind * share:(kind + 1) * share] = kept[:, d * share:(d + 1) * share]
     pl.semaphore_wait(barrier, n_mp - 1 + n_seq - 1 + 1)
 
     def mod_copy(k):
@@ -119,29 +122,60 @@
             src_ref=mod_all.at[origin], dst_ref=mod_all.at[origin], send_sem=mod_send.at[k],
             recv_sem=mod_recv.at[k], device_id=at(section, seq, origin), device_id_type=MESH)
 
-    def stale_copy(k, origin):
-        return pltpu.make_async_remote_copy(
-            src_ref=stale_all.at[origin], dst_ref=stale_all.at[origin], send_sem=stale_send.at[k],
-            recv_sem=stale_recv.at[k], device_id=at(section, lax.rem(seq + k, n_seq), mp), device_id_type=MESH)
+    def to_device(send, recv, sems, d):
+        return pltpu.make_async_remote_copy(
+            src_ref=send.at[d], dst_ref=recv.at[seq], send_sem=sems[0].at[d], recv_sem=sems[1].at[seq],
+            device_id=at(section, d, mp), device_id_type=MESH)
+
+    def from_device(send, recv, sems, origin):
+        return pltpu.make_async_remote_copy(
+            src_ref=recv.at[origin], dst_ref=recv.at[origin], send_sem=sems[0].at[origin], recv_sem=sems[1].at[origin],
+            device_id=at(section, origin, mp), device_id_type=MESH)
+
+    def send_part(exchange, d):
+        @pl.when(seq != d)
+        def _():
+            to_device(*exchange, d).start()
+
+    def keep_part(exchange, d):
+        @pl.when(seq == d)
+        def _():
+            exchange[1][d] = exchange[0][d]
+
+    def sent_part(exchange, d):
+        @pl.when(seq != d)
+        def _():
+            to_device(*exchange, d).wait_send()
+
+    stale_exchange = (stale_send_buf, stale_recv_buf, (stale_send, stale_recv))
+    heads_exchange = (heads_send, heads_recv, (heads_out, heads_in))
+    back_exchange = (back_send, back_recv, (back_out, back_in))
+
+    def when_active(function):
+        if active == n_seq:
+            function()
+        else:
+            pl.when(seq < active)(function)
 
     for k in range(1, n_mp):
         mod_copy(k).start()
-    for k in range(1, n_seq):
-        stale_copy(k, seq).start()
-
-    row_head, row_index = split_index((2 * rows, 1), 0, rows, 2)
+    for d in range(active):
+        send_part(stale_exchange, d)
+        keep_part(stale_exchange, d)
+
+    row_index = lax.broadcasted_iota(jnp.int32, (rows, 1), 0)
     row_req, row_patch, _ = slot_marks(
-        row_index, lengths_ref, text_len_ref, requests, 0, patches, per_dev, text_dev, row_head)
+        row_index, lengths_ref, text_len_ref, requests, 0, patches, per_dev, text_dev, 0)
     key_owner, key_index = split_index((1, n_seq * rows), 1, rows, n_seq)
     key_req, key_patch, key_live = slot_marks(
         key_index, lengths_ref, text_len_ref, requests, 0, patches, per_dev, text_dev, key_owner)
     key_limit = jnp.where(key_live, key_patch, patches)
-    bias_f[...] = jnp.where((row_req == key_req) & (key_limit <= row_patch), 0.0, NEG)
+    bias[:, :fresh_keys] = jnp.where((row_req == key_req) & (key_limit <= row_patch), 0.0, NEG)
     key_owner, key_index = split_index((1, n_seq * stale_rows), 1, stale_rows, n_seq)
     key_req, key_patch, key_live = slot_marks(
         key_index, lengths_ref, text_len_ref, requests, 1, patches, per_dev, 0, key_owner)
     key_limit = jnp.where(key_live, key_patch, -1)
-    bias_s[...] = jnp.where((row_req == key_req) & (key_limit > row_patch), 0.0, NEG)
+    bias[:, fresh_keys:] = jnp.where((row_req == key_req) & (key_limit > row_patch), 0.0, NEG)
 
     @pl.when(section == 0)
     def _():
@@ -203,66 +237,75 @@
         piece_values = (x_buf[:, span].astype(F32) - mean) * inverse
         normed[:, span] = (piece_values * (1.0 + modulated(n_mp + c)) + modulated(c)).astype(BF16)
 
-    def kv_copy(g, k, origin):
-        return pltpu.make_async_remote_copy(
-            src_ref=kv_all.at[g, origin], dst_ref=kv_all.at[g, origin], send_sem=kv_send.at[g, k],
-            recv_sem=kv_recv.at[g, k], device_id=at(section, lax.rem(seq + k, n_seq), mp), device_id_type=MESH)
-
     def project(part, g):
         return jnp.dot(normed[...], w_qkv[part, :, g * GROUP:(g + 1) * GROUP], preferred_element_type=F32)
 
-    for copy in weight_copies[1:1 + pieces]:
-        copy.wait()
-    for g in range(groups):
-        key = project(1, g).astype(BF16)
-        if g == 0:
-            for copy in weight_copies[1 + pieces:1 + 2 * pieces]:
-                copy.wait()
-        value = project(2, g).astype(BF16)
-        kv_all[g, seq, :, 0:GROUP] = key
-        kv_all[g, seq, :, GROUP:2 * GROUP] = value
-        for k in range(1, n_seq):
-            kv_copy(g, k, seq).start()
-    for copy in weight_copies[1 + 2 * pieces:1 + 3 * pieces]:
-        copy.wait()
-    for g in range(groups):
-        query[:, g * GROUP:(g + 1) * GROUP] = (project(0, g).astype(BF16).astype(F32) * HEAD ** (-0.5)).astype(BF16)
+    order = []
+    for t in range(groups):
+        order.insert(t, groups - 1 - t // 2 if t % 2 else t // 2)
+    done, sent = set(), set()
+    for g in order:
+        for part in (1, 2, 0):
+            if g == order[0]:
+                at_piece = 1 + (1, 2, 0).index(part) * pieces
+                for copy in weight_copies[at_piece:at_piece + pieces]:
+                    copy.wait()
+            tile = project(part, g).astype(BF16)
+            if part == 0:
+                tile = (tile.astype(F32) * HEAD ** (-0.5)).astype(BF16)
+            projected[part, :, g * GROUP:(g + 1) * GROUP] = tile
+        done.add(g)
+        for d in range(active):
+            first, last = d * share // GROUP, ((d + 1) * share - 1) // GROUP
+            if d not in sent and all(t in done for t in range(first, last + 1)):
+                sent.add(d)
+                for part in range(3):
+                    heads_send[d, :, part * share:(part + 1) * share] = projected[part, :, d * share:(d + 1) * share]
+                send_part(heads_exchange, d)
+                keep_part(heads_exchange, d)
 
     for g in range(groups):
         for kind in range(2):
             span = slice(g * GROUP, (g + 1) * GROUP)
-            part = kv_all[g, seq, :, kind * GROUP:(kind + 1) * GROUP]
+            part = projected[1 + kind, :, span]
             cache_video[:, kind, span] = part[:video_rows]
             cache_text[:, kind, span] = part[video_rows:]
 
-    for k in range(1, n_seq):
-        stale_copy(k, lax.rem(seq + n_seq - k, n_seq)).wait_recv()
-    low = lax.broadcasted_iota(jnp.int32, (rows, SLAB), 1) < HEAD
-    contract_last = (((1,), (1,)), ((), ()))
-    for g in range(groups):
+    @when_active
+    def _():
         for k in range(1, n_seq):
-            kv_copy(g, k, lax.rem(seq + n_seq - k, n_seq)).wait_recv()
-        for h in range(GROUP // SLAB):
-            span = slice(g * GROUP + h * SLAB, g * GROUP + (h + 1) * SLAB)
-            k_span = slice(h * SLAB, (h + 1) * SLAB)
-            v_span = slice(GROUP + h * SLAB, GROUP + (h + 1) * SLAB)
-            slab = query[:, span]
-            zero = jnp.zeros_like(slab)
-            pair = jnp.concatenate([jnp.where(low, slab, zero), jnp.where(low, zero, slab)], axis=0)
-            fresh_k = kv_all[g, :, :, k_span].reshape(n_seq * rows, SLAB)
-            fresh_v = kv_all[g, :, :, v_span].reshape(n_seq * rows, SLAB)
-            stale_k = stale_all[:, g, :, k_span].reshape(n_seq * stale_rows, SLAB)
-            stale_v = stale_all[:, g, :, v_span].reshape(n_seq * stale_rows, SLAB)
-            s_f = lax.dot_general(pair, fresh_k, contract_last, preferred_element_type=F32) + bias_f[...]
-            s_s = lax.dot_general(pair, stale_k, contract_last, preferred_element_type=F32) + bias_s[...]
-            top = jnp.maximum(jnp.max(s_f, axis=-1, keepdims=True), jnp.max(s_s, axis=-1, keepdims=True))
-            e_f = jnp.exp(s_f - top)
-            e_s = jnp.exp(s_s - top)
-            total = jnp.sum(e_f, axis=-1, keepdims=True) + jnp.sum(e_s, axis=-1, keepdims=True)
-            mixed = jnp.dot(e_f.astype(BF16), fresh_v, preferred_element_type=F32)
-            mixed = mixed + jnp.dot(e_s.astype(BF16), stale_v, preferred_element_type=F32)
-            mixed = mixed / total
-            attended[:, span] = jnp.where(low, mixed[:rows], mixed[rows:]).astype(BF16)
+            from_device(*stale_exchange, lax.rem(seq + n_seq - k, n_seq)).wait_recv()
+        for h in range(each):
+            for kind, cat in enumerate((key_cat, value_cat)):
+                at_col = kind * share + h * HEAD
+                cat[h, fresh_keys:] = stale_recv_buf[:, :, at_col:at_col + HEAD].reshape(n_seq * stale_rows, HEAD)
+        for k in range(1, n_seq):
+            from_device(*heads_exchange, lax.rem(seq + n_seq - k, n_seq)).wait_recv()
+        for h in range(each):
+            for kind, cat in enumerate((key_cat, value_cat)):
+                at_col = (1 + kind) * share + h * HEAD
+                cat[h, :fresh_keys] = heads_recv[:, :, at_col:at_col + HEAD].reshape(fresh_keys, HEAD)
+        for i in range(n_seq):
+            d = n_seq - 1 - i // 2 if i % 2 else i // 2
+            for h in range(each):
+                heads_at = slice(h * HEAD, (h + 1) * HEAD)
+                scores = lax.dot_general(
+                    heads_recv[d, :, heads_at], key_cat[h], (((1,), (1,)), ((), ())), preferred_element_type=F32)
+                scores = scores + bias[...]
+                top = jnp.max(scores, axis=-1, keepdims=True)
+                weights = jnp.exp(scores - top)
+                total = jnp.sum(weights, axis=-1, keepdims=True)
+                mixed = jnp.dot(weights.astype(BF16), value_cat[h], preferred_element_type=F32)
+                back_send[d, :, heads_at] = (mixed / total).astype(BF16)
+            send_part(back_exchange, d)
+            keep_part(back_exchange, d)
+
+    for d in range(active):
+        @pl.when(seq != d)
+        def _():
+            from_device(*back_exchange, d).wait_recv()
+    for d in range(active):
+        attended[:, d * share:(d + 1) * share] = back_recv[d, :, :share]
 
     def part_copy(k):
         return pltpu.make_async_remote_copy(
@@ -316,19 +359,38 @@
         mod_copy(k).wait_send()
     for k in range(3):
         part_copy(k).wait_send()
-    for k in range(1, n_seq):
-        stale_copy(k, seq).wait_send()
-        for g in range(groups):
-            kv_copy(g, k, seq).wait_send()
+    for d in range(active):
+        sent_part(stale_exchange, d)
+        sent_part(heads_exchange, d)
+
+    @when_active
+    def _():
+        for d in range(n_seq):
+            sent_part(back_exchange, d)
 
 
 def store_kernel(*refs):
-    sems = refs[-1]
-    copies = [pltpu.make_async_copy(refs[i], refs[4 + i], sems.at[i]) for i in range(4)]
-    for copy in copies:
+    ins, outs, held, sems = refs[:4], refs[4:8], refs[8:12], refs[12]
+    loads = [pltpu.make_async_copy(ins[i], held[i], sems.at[0, i]) for i in range(4)]
+    stores = [pltpu.make_async_copy(held[i], outs[i], sems.at[1, i]) for i in range(4)]
+    for copy in loads:
         copy.start()
-    for copy in copies:
+    for load, store in zip(loads, stores):
+        load.wait()
+        store.start()
+    for copy in stores:
         copy.wait()
+
+
+def padded(count):
+    return -(-count // SLAB) * SLAB
+
+
+def head_split(heads, n_seq):
+    each = -(-heads // n_seq)
+    while heads % each:
+        each += 1
+    return each, heads // each
 
 
 def body(video, text, patch_lengths, text_len, timestep, w_mod, w_qkv, w_out, stale_cache):
@@ -336,7 +398,8 @@
     requests, patches, per_dev, width = video.shape
     text_dev = text.shape[1]
     cols = w_out.shape[1]
-    groups = cols // GROUP
+    each, active = head_split(cols // HEAD, n_seq)
+    share = each * HEAD
     rows = requests * (patches * per_dev + text_dev)
     video_rows = requests * patches * per_dev
     text_rows = requests * text_dev
@@ -346,9 +409,10 @@
     frequency = jnp.exp(-math.log(10000.0) * jnp.arange(half_width, dtype=F32) / half_width)
     phases = timestep.astype(F32)[0] * frequency
     embedding = jnp.concatenate([jnp.cos(phases), jnp.sin(phases)])
-    active = jax.nn.silu(embedding).astype(BF16)
+    act = jax.nn.silu(embedding).astype(BF16)
 
     mod_cols = w_mod.shape[2]
+    keys = n_seq * (rows + stale_rows)
     dims = (requests, patches, per_dev, text_dev, n_seq, n_mp, width, cols)
     vmem = pl.BlockSpec(memory_space=pltpu.VMEM)
     smem = pl.BlockSpec(memory_space=pltpu.SMEM)
@@ -370,20 +434,26 @@
             pltpu.VMEM((cols, width), BF16),
             pltpu.VMEM((rows, width), BF16),
             pltpu.VMEM((rows, width), BF16),
-            pltpu.VMEM((rows, cols), BF16),
+            pltpu.VMEM((3, rows, cols), BF16),
             pltpu.VMEM((rows, cols), BF16),
             pltpu.VMEM((rows, width), BF16),
             pltpu.VMEM((n_mp, 8, mod_cols), F32),
-            pltpu.VMEM((groups, n_seq, rows, 2 * GROUP), BF16),
-            pltpu.VMEM((n_seq, groups, stale_rows, 2 * GROUP), BF16),
+            pltpu.VMEM((active, rows, padded(3 * share)), BF16),
+            pltpu.VMEM((n_seq, rows, padded(3 * share)), BF16),
+            pltpu.VMEM((n_seq, rows, padded(share)), BF16),
+            pltpu.VMEM((n_seq, rows, padded(share)), BF16),
+            pltpu.VMEM((active, stale_rows, padded(2 * share)), BF16),
+            pltpu.VMEM((n_seq, stale_rows, padded(2 * share)), BF16),
+            pltpu.VMEM((each, keys, HEAD), BF16),
+            pltpu.VMEM((each, keys, HEAD), BF16),
             pltpu.VMEM((3, rows, cols), BF16),
             pltpu.VMEM((3, rows, cols), BF16),
-            pltpu.VMEM((2 * rows, n_seq * rows), F32),
-            pltpu.VMEM((2 * rows, n_seq * stale_rows), F32),
+            pltpu.VMEM((rows, keys), F32),
             dma((11,)),
             dma((n_mp,)), dma((n_mp,)),
             dma((n_seq,)), dma((n_seq,)),
-            dma((groups, n_seq)), dma((groups, n_seq)),
+            dma((n_seq,)), dma((n_seq,)),
+            dma((n_seq,)), dma((n_seq,)),
             dma((n_mp,)), dma((n_mp,)),
             dma((2,)), dma((2,)),
             dma((2, 3)), dma((2, 3)),
@@ -397,7 +467,7 @@
         ),
         name="layer",
     )(
-        patch_lengths, text_len, active[None, :],
+        patch_lengths, text_len, act[None, :],
         video.reshape(video_rows, width), text.reshape(text_rows, width), stale_cache.reshape(video_rows, 2, cols),
         w_mod[0], w_qkv[0].transpose(1, 0, 2), w_out[0],
     )
@@ -406,7 +476,7 @@
         out_shape=tuple(jax.ShapeDtypeStruct(o.shape, o.dtype) for o in outputs),
         in_specs=[hbm] * 4,
         out_specs=(hbm,) * 4,
-        scratch_shapes=[dma((4,))],
+        scratch_shapes=[pltpu.VMEM(o.shape, o.dtype) for o in outputs] + [dma((2, 4))],
         compiler_params=pltpu.CompilerParams(vmem_limit_bytes=56 * 1024 * 1024),
         name="store",
     )(*outputs)

time: 118 us -> 80.7 us (0.68); the launches traced: 116 us -> 80.6 us
  Pallas kernels: 114 us -> 78.6 us
    pallas_call x1, Pallas kernels: 23.5 us -> 1.91 us  [body(): pl.pallas_call(store_kernel, out_shape=tuple((jax.ShapeDtypeStruct(o.shap...]
    pallas_call x1, Pallas kernels: 90.8 us -> 76.7 us  [body(): pl.pallas_call(functools.partial(kernel, dims), out_shape=(jax.ShapeDtype...]
where the time goes in v3:
time: 80.7 us; the launch traced here: 80.6 us
  Pallas kernels  78.6 us (97%)
  between operations  1.29 us (2%)
    pallas_call x1, Pallas kernels, body(): pl.pallas_call(functools.partial(kernel, dims), out_shape=(jax.ShapeDtype...  76.7 us
    pallas_call x1, Pallas kernels, body(): pl.pallas_call(store_kernel, out_shape=tuple((jax.ShapeDtypeStruct(o.shap...  1.91 us

profile of v3, /device:TPU:3, one launch (start us, length us, event | category | flops | bytes accessed | tf_op | source)
XLA Modules:
  0.0 80.6 jit_solution(14500823476702769052)
XLA Ops:
  1.3 0.6 fusion.act_ref
  1.9 76.7 %layer.1 = (bf16[64,3072]{1,0:T(8,128)(2,1)}, bf16[16,3072]{1,0:T(8,128)(2,1)}, bf16[64,2,768]{2,1,0:T(2,128)(2,1)}, bf16[16,2,768]{2,1,0:T(2,128)(2,1)}) custom-call(s32[2,4]{1,0:T(2,128)} %lengths_ref.1, s32[2]{0:T(128)} %text_len_ref.1, bf16[1,512]{1,0:T(2,128)(2,1)} %fusion.act_ref, bf16[64,3072]{1,0:T(8,128)(2,1)} %bitcast.18, ...), custom_call_target="tpu_custom_call" | custom-call | flops 1509949440 | bytes 22020096 | tf_op jit(solution)/shard_map/layer/pallas_call | solution.py:421
  78.6 1.9 %store.1 = (bf16[64,3072]{1,0:T(8,128)(2,1)}, bf16[16,3072]{1,0:T(8,128)(2,1)}, bf16[64,2,768]{2,1,0:T(2,128)(2,1)}, bf16[16,2,768]{2,1,0:T(2,128)(2,1)}) custom-call(bf16[64,3072]{1,0:T(8,128)(2,1)} %get-tuple-element.12.refs_0_, bf16[16,3072]{1,0:T(8,128)(2,1)} %get-tuple-element.13.refs_1_, bf16[64,2,768]{2,1,0:T(2,128)(2,1)} %get-tuple-element.14.refs_2_, ...), custom_call_target="tpu_custom_call" | custom-call | tf_op jit(solution)/shard_map/store/pallas_call | solution.py:474
  (1 shorter events, 0.0 us)

commit v4 on v3

--- a/solution.py
+++ b/solution.py
@@ -75,11 +75,19 @@
     diagonal = lax.rem(core_mate + 2, n_mp)
     half = rows // 32 * 16 + 16 * (rows // 16 % 2)
     row_pieces = (pl.ds(0, half), pl.ds(half, rows - half))
+    row_slices = (slice(0, half), slice(half, rows))
 
     def at(sec, se, m):
         return (sec, se, m)
 
-    weight_copies = [pltpu.make_async_copy(w_mod_hbm, w_mod, w_sem.at[0])]
+    mod_pieces = 4
+    mod_piece = w_mod.shape[0] // mod_pieces
+    mod_weights = [
+        pltpu.make_async_copy(w_mod_hbm.at[pl.ds(i * mod_piece, mod_piece)], w_mod.at[pl.ds(i * mod_piece, mod_piece)],
+                              w_sem.at[11 + i]) for i in range(mod_pieces)]
+    for copy in mod_weights:
+        copy.start()
+    weight_copies = []
     pieces = 3
     piece = width // pieces
     for part in (1, 2, 0):
@@ -89,9 +97,6 @@
                 w_qkv.at[part, pl.ds(i * piece, piece)],
                 w_sem.at[1 + part * pieces + i]))
     weight_copies.append(pltpu.make_async_copy(w_out_hbm, w_out, w_sem.at[1 + 3 * pieces]))
-    for copy in weight_copies:
-        copy.start()
-
     barrier = pltpu.get_barrier_semaphore()
     for k in range(1, n_mp):
         pl.semaphore_signal(barrier, inc=1, device_id=at(section, seq, lax.rem(mp + k, n_mp)), device_id_type=MESH)
@@ -99,9 +104,63 @@
         pl.semaphore_signal(barrier, inc=1, device_id=at(section, lax.rem(seq + k, n_seq), mp), device_id_type=MESH)
     pl.semaphore_signal(barrier, inc=1, device_id=at(other, seq, mp), device_id_type=MESH)
 
-    weight_copies[0].wait()
+    for copy in mod_weights:
+        copy.wait()
+    for copy in weight_copies:
+        copy.start()
     act = jnp.broadcast_to(act_ref[...].astype(F32), (8, act_ref.shape[1])).astype(BF16)
     mod_all[mp] = jnp.dot(act, w_mod[...], preferred_element_type=F32)
+    pl.semaphore_wait(barrier, n_mp - 1 + n_seq - 1 + 1)
+
+    def mod_copy(k):
+        return pltpu.make_async_remote_copy(
+            src_ref=mod_all.at[mp], dst_ref=mod_all.at[mp], send_sem=mod_send.at[k],
+            recv_sem=mod_recv.at[k], device_id=at(section, seq, lax.rem(mp + k, n_mp)), device_id_type=MESH)
+
+    def mod_arrival(k):
+        origin = lax.rem(mp + n_mp - k, n_mp)
+        return pltpu.make_async_remote_copy(
+            src_ref=mod_all.at[origin], dst_ref=mod_all.at[origin], send_sem=mod_send.at[k],
+            recv_sem=mod_recv.at[k], device_id=at(section, seq, origin), device_id_type=MESH)
+
+    def to_device(send, recv, sems, d):
+        return pltpu.make_async_remote_copy(
+            src_ref=send.at[d], dst_ref=recv.at[seq], send_sem=sems[0].at[d], recv_sem=sems[1].at[seq],
+            device_id=at(section, d, mp), device_id_type=MESH)
+
+    def from_device(send, recv, sems, origin):
+        return pltpu.make_async_remote_copy(
+            src_ref=recv.at[origin], dst_ref=recv.at[origin], send_sem=sems[0].at[origin], recv_sem=sems[1].at[origin],
+            device_id=at(section, origin, mp), device_id_type=MESH)
+
+    def send_part(exchange, d):
+        @pl.when(seq != d)
+        def _():
+            to_device(*exchange, d).start()
+
+    def keep_part(exchange, d):
+        @pl.when(seq == d)
+        def _():
+            exchange[1][d] = exchange[0][d]
+
+    def sent_part(exchange, d):
+        @pl.when(seq != d)
+        def _():
+            to_device(*exchange, d).wait_send()
+
+    stale_exchange = (stale_send_buf, stale_recv_buf, (stale_send, stale_recv))
+    heads_exchange = (heads_send, heads_recv, (heads_out, heads_in))
+    back_exchange = (back_send, back_recv, (back_out, back_in))
+
+    def when_active(function):
+        if active == n_seq:
+            function()
+        else:
+            pl.when(seq < active)(function)
+
+    for k in range(1, n_mp):
+        mod_copy(k).start()
+
     span_all = patches * per_dev
     for kind in range(2):
         whole = stale_ref[:, kind, :].astype(F32)
@@ -109,56 +168,6 @@
             [whole[r * span_all + per_dev:(r + 1) * span_all] for r in range(requests)], axis=0).astype(BF16)
         for d in range(active):
             stale_send_buf[d, :, kind * share:(kind + 1) * share] = kept[:, d * share:(d + 1) * share]
-    pl.semaphore_wait(barrier, n_mp - 1 + n_seq - 1 + 1)
-
-    def mod_copy(k):
-        return pltpu.make_async_remote_copy(
-            src_ref=mod_all.at[mp], dst_ref=mod_all.at[mp], send_sem=mod_send.at[k],
-            recv_sem=mod_recv.at[k], device_id=at(section, seq, lax.rem(mp + k, n_mp)), device_id_type=MESH)
-
-    def mod_arrival(k):
-        origin = lax.rem(mp + n_mp - k, n_mp)
-        return pltpu.make_async_remote_copy(
-            src_ref=mod_all.at[origin], dst_ref=mod_all.at[origin], send_sem=mod_send.at[k],
-            recv_sem=mod_recv.at[k], device_id=at(section, seq, origin), device_id_type=MESH)
-
-    def to_device(send, recv, sems, d):
-        return pltpu.make_async_remote_copy(
-            src_ref=send.at[d], dst_ref=recv.at[seq], send_sem=sems[0].at[d], recv_sem=sems[1].at[seq],
-            device_id=at(section, d, mp), device_id_type=MESH)
-
-    def from_device(send, recv, sems, origin):
-        return pltpu.make_async_remote_copy(
-            src_ref=recv.at[origin], dst_ref=recv.at[origin], send_sem=sems[0].at[origin], recv_sem=sems[1].at[origin],
-            device_id=at(section, origin, mp), device_id_type=MESH)
-
-    def send_part(exchange, d):
-        @pl.when(seq != d)
-        def _():
-            to_device(*exchange, d).start()
-
-    def keep_part(exchange, d):
-        @pl.when(seq == d)
-        def _():
-            exchange[1][d] = exchange[0][d]
-
-    def sent_part(exchange, d):
-        @pl.when(seq != d)
-        def _():
-            to_device(*exchange, d).wait_send()
-
-    stale_exchange = (stale_send_buf, stale_recv_buf, (stale_send, stale_recv))
-    heads_exchange = (heads_send, heads_recv, (heads_out, heads_in))
-    back_exchange = (back_send, back_recv, (back_out, back_in))
-
-    def when_active(function):
-        if active == n_seq:
-            function()
-        else:
-            pl.when(seq < active)(function)
-
-    for k in range(1, n_mp):
-        mod_copy(k).start()
     for d in range(active):
         send_part(stale_exchange, d)
         keep_part(stale_exchange, d)
@@ -215,9 +224,6 @@
 
     x_sems, result_sems = (x_send, x_recv), (res_send, res_recv)
 
-    for k in range(1, n_mp):
-        mod_arrival(k).wait_recv()
-
     @pl.when(section == 1)
     def _():
         for c in range(2):
@@ -232,6 +238,8 @@
     mean = jnp.mean(values, axis=-1, keepdims=True)
     center = values - mean
     inverse = lax.rsqrt(jnp.mean(center * center, axis=-1, keepdims=True) + EPS)
+    for k in range(1, n_mp):
+        mod_arrival(k).wait_recv()
     for c in range(n_mp):
         span = slice(c * cols, (c + 1) * cols)
         piece_values = (x_buf[:, span].astype(F32) - mean) * inverse
@@ -240,29 +248,38 @@
     def project(part, g):
         return jnp.dot(normed[...], w_qkv[part, :, g * GROUP:(g + 1) * GROUP], preferred_element_type=F32)
 
-    order = []
-    for t in range(groups):
-        order.insert(t, groups - 1 - t // 2 if t % 2 else t // 2)
-    done, sent = set(), set()
-    for g in order:
-        for part in (1, 2, 0):
-            if g == order[0]:
-                at_piece = 1 + (1, 2, 0).index(part) * pieces
-                for copy in weight_copies[at_piece:at_piece + pieces]:
-                    copy.wait()
-            tile = project(part, g).astype(BF16)
-            if part == 0:
-                tile = (tile.astype(F32) * HEAD ** (-0.5)).astype(BF16)
-            projected[part, :, g * GROUP:(g + 1) * GROUP] = tile
-        done.add(g)
-        for d in range(active):
-            first, last = d * share // GROUP, ((d + 1) * share - 1) // GROUP
-            if d not in sent and all(t in done for t in range(first, last + 1)):
-                sent.add(d)
-                for part in range(3):
-                    heads_send[d, :, part * share:(part + 1) * share] = projected[part, :, d * share:(d + 1) * share]
-                send_part(heads_exchange, d)
-                keep_part(heads_exchange, d)
+    middle = (n_seq + 1) // 2
+    lower = 1 - seq // middle
+
+    def project_all(order):
+        done, sent = set(), set()
+        for g in order:
+            for index, part in enumerate((1, 2, 0)):
+                if g == order[0]:
+                    for copy in weight_copies[index * pieces:(index + 1) * pieces]:
+                        copy.wait()
+                tile = project(part, g).astype(BF16)
+                if part == 0:
+                    tile = (tile.astype(F32) * HEAD ** (-0.5)).astype(BF16)
+                projected[part, :, g * GROUP:(g + 1) * GROUP] = tile
+            done.add(g)
+            for d in sorted(range(active), reverse=order[0] != 0):
+                first, last = d * share // GROUP, ((d + 1) * share - 1) // GROUP
+                if d not in sent and all(t in done for t in range(first, last + 1)):
+                    sent.add(d)
+                    for part in range(3):
+                        heads_send[d, :, part * share:(part + 1) * share] = (
+                            projected[part, :, d * share:(d + 1) * share])
+                    send_part(heads_exchange, d)
+                    keep_part(heads_exchange, d)
+
+    @pl.when(lower == 1)
+    def _():
+        project_all(tuple(reversed(range(groups))))
+
+    @pl.when(lower == 0)
+    def _():
+        project_all(tuple(range(groups)))
 
     for g in range(groups):
         for kind in range(2):
@@ -286,7 +303,7 @@
                 at_col = (1 + kind) * share + h * HEAD
                 cat[h, :fresh_keys] = heads_recv[:, :, at_col:at_col + HEAD].reshape(fresh_keys, HEAD)
         for i in range(n_seq):
-            d = n_seq - 1 - i // 2 if i % 2 else i // 2
+            d = i + lower * (n_seq - 1 - 2 * i)
             for h in range(each):
                 heads_at = slice(h * HEAD, (h + 1) * HEAD)
                 scores = lax.dot_general(
@@ -310,7 +327,13 @@
     def part_copy(k):
         return pltpu.make_async_remote_copy(
             src_ref=part_send.at[k], dst_ref=part_recv.at[k], send_sem=p_send.at[k], recv_sem=p_recv.at[k],
-            device_id=at(section, seq, y_mate if k == 2 else core_mate), device_id_type=MESH)
+            device_id=at(section, seq, core_mate), device_id_type=MESH)
+
+    def y_copy(c):
+        return pltpu.make_async_remote_copy(
+            src_ref=part_send.at[2, row_pieces[c]], dst_ref=part_recv.at[2, row_pieces[c]],
+            send_sem=p_send.at[2 + c], recv_sem=p_recv.at[2 + c],
+            device_id=at(section, seq, y_mate), device_id_type=MESH)
 
     weight_copies[-1].wait()
 
@@ -321,25 +344,27 @@
     part_copy(0).start()
     passed = out_block(y_mate)
     part_copy(0).wait_recv()
-    part_send[2] = (passed + part_recv[0].astype(F32)).astype(BF16)
-    part_copy(2).start()
+    for c in range(2):
+        at_rows = row_slices[c]
+        part_send[2, at_rows] = (passed[at_rows] + part_recv[0, at_rows].astype(F32)).astype(BF16)
+        y_copy(c).start()
     part_send[1] = out_block(core_mate).astype(BF16)
     part_copy(1).start()
     summed = out_block(mp)
     part_copy(1).wait_recv()
     summed = summed + part_recv[1].astype(F32)
-    part_copy(2).wait_recv()
-    summed = summed + part_recv[2].astype(F32)
     gate_at = 2 * n_mp + mp
     gate = mod_all[gate_at // 3, 0:1, pl.ds(pl.multiple_of(gate_at % 3 * cols, SLAB), cols)]
-    result[:, block(mp)] = (x_buf[:, block(mp)].astype(F32) + gate * summed).astype(BF16)
-
-    @pl.when(section == 0)
-    def _():
-        for c in range(2):
+    for c in range(2):
+        at_rows = row_slices[c]
+        y_copy(c).wait_recv()
+        whole_sum = summed[at_rows] + part_recv[2, at_rows].astype(F32)
+        result[at_rows, block(mp)] = (x_buf[at_rows, block(mp)].astype(F32) + gate * whole_sum).astype(BF16)
+
+        @pl.when(section == 0)
+        def _():
             cross_copy(c).start()
 
-    for c in range(2):
         spread_start(result, result_sems, c)
     spread_finish(result, result_sems)
     hidden_video[...] = result[pl.ds(0, video_rows)]
@@ -357,8 +382,9 @@
     spread_sent(result, result_sems)
     for k in range(1, n_mp):
         mod_copy(k).wait_send()
-    for k in range(3):
+    for k in range(2):
         part_copy(k).wait_send()
+        y_copy(k).wait_send()
     for d in range(active):
         sent_part(stale_exchange, d)
         sent_part(heads_exchange, d)
@@ -449,12 +475,12 @@
             pltpu.VMEM((3, rows, cols), BF16),
             pltpu.VMEM((3, rows, cols), BF16),
             pltpu.VMEM((rows, keys), F32),
-            dma((11,)),
+            dma((15,)),
             dma((n_mp,)), dma((n_mp,)),
             dma((n_seq,)), dma((n_seq,)),
             dma((n_seq,)), dma((n_seq,)),
             dma((n_seq,)), dma((n_seq,)),
-            dma((n_mp,)), dma((n_mp,)),
+            dma((4,)), dma((4,)),
             dma((2,)), dma((2,)),
             dma((2, 3)), dma((2, 3)),
             dma((2, 3)), dma((2, 3)),

time: 80.7 us -> 76.7 us (0.950)
  Pallas kernels: 78.6 us -> 74.5 us
    pallas_call x1, Pallas kernels: 76.7 us -> 72.6 us  [body(): pl.pallas_call(functools.partial(kernel, dims), out_shape=(jax.ShapeDtype...]
where the time goes in v4:
time: 76.7 us; the launch traced here: 76.5 us
  Pallas kernels  74.5 us (97%)
  between operations  1.29 us (2%)
    pallas_call x1, Pallas kernels, body(): pl.pallas_call(functools.partial(kernel, dims), out_shape=(jax.ShapeDtype...  72.6 us
    pallas_call x1, Pallas kernels, body(): pl.pallas_call(store_kernel, out_shape=tuple((jax.ShapeDtypeStruct(o.shap...  1.91 us

profile of v4, /device:TPU:3, one launch (start us, length us, event | category | flops | bytes accessed | tf_op | source)
XLA Modules:
  0.0 76.5 jit_solution(9550514662892360131)
XLA Ops:
  1.3 0.6 fusion.act_ref
  1.9 72.6 %layer.1 = (bf16[64,3072]{1,0:T(8,128)(2,1)}, bf16[16,3072]{1,0:T(8,128)(2,1)}, bf16[64,2,768]{2,1,0:T(2,128)(2,1)}, bf16[16,2,768]{2,1,0:T(2,128)(2,1)}) custom-call(s32[2,4]{1,0:T(2,128)} %lengths_ref.1, s32[2]{0:T(128)} %text_len_ref.1, bf16[1,512]{1,0:T(2,128)(2,1)} %fusion.act_ref, bf16[64,3072]{1,0:T(8,128)(2,1)} %bitcast.18, ...), custom_call_target="tpu_custom_call" | custom-call | flops 1509949440 | bytes 22020096 | tf_op jit(solution)/shard_map/layer/pallas_call | solution.py:447
  74.6 1.9 %store.1 = (bf16[64,3072]{1,0:T(8,128)(2,1)}, bf16[16,3072]{1,0:T(8,128)(2,1)}, bf16[64,2,768]{2,1,0:T(2,128)(2,1)}, bf16[16,2,768]{2,1,0:T(2,128)(2,1)}) custom-call(bf16[64,3072]{1,0:T(8,128)(2,1)} %get-tuple-element.12.refs_0_, bf16[16,3072]{1,0:T(8,128)(2,1)} %get-tuple-element.13.refs_1_, bf16[64,2,768]{2,1,0:T(2,128)(2,1)} %get-tuple-element.14.refs_2_, ...), custom_call_target="tpu_custom_call" | custom-call | tf_op jit(solution)/shard_map/store/pallas_call | solution.py:500
  (1 shorter events, 0.0 us)

commit v5 on v4

--- a/solution.py
+++ b/solution.py
@@ -55,9 +55,9 @@
 def kernel(dims, lengths_ref, text_len_ref, act_ref, video_ref, text_ref, stale_ref, w_mod_hbm,
            w_qkv_hbm, w_out_hbm, hidden_video, hidden_text, cache_video, cache_text,
            w_mod, w_qkv, w_out, x_buf, normed, projected, attended, result, mod_all, heads_send, heads_recv,
-           back_send, back_recv, stale_send_buf, stale_recv_buf, key_cat, value_cat, part_send, part_recv, bias,
+           back_send, back_recv, stale_held, cache_held, stale_send_buf, stale_recv_buf, key_cat, value_cat, part_send, part_recv, bias,
            w_sem, mod_send, mod_recv, stale_send, stale_recv, heads_out, heads_in, back_out, back_in, p_send, p_recv,
-           cross_send, cross_recv, x_send, x_recv, res_send, res_recv):
+           cross_send, cross_recv, x_send, x_recv, res_send, res_recv, in_sem, out_sem):
     requests, patches, per_dev, text_dev, n_seq, n_mp, width, cols = dims
     rows = requests * (patches * per_dev + text_dev)
     video_rows = requests * patches * per_dev
@@ -87,6 +87,22 @@
                               w_sem.at[11 + i]) for i in range(mod_pieces)]
     for copy in mod_weights:
         copy.start()
+    in_copies = [
+        pltpu.make_async_copy(video_ref, x_buf.at[pl.ds(0, video_rows)], in_sem.at[0]),
+        pltpu.make_async_copy(text_ref, x_buf.at[pl.ds(video_rows, rows - video_rows)], in_sem.at[1]),
+        pltpu.make_async_copy(stale_ref, stale_held, in_sem.at[2])]
+    out_copies = [
+        pltpu.make_async_copy(result.at[pl.ds(0, video_rows)], hidden_video, out_sem.at[0]),
+        pltpu.make_async_copy(result.at[pl.ds(video_rows, rows - video_rows)], hidden_text, out_sem.at[1]),
+        pltpu.make_async_copy(cache_held.at[pl.ds(0, video_rows)], cache_video, out_sem.at[2]),
+        pltpu.make_async_copy(cache_held.at[pl.ds(video_rows, rows - video_rows)], cache_text, out_sem.at[3])]
+    in_copies[2].start()
+
+    @pl.when(section == 0)
+    def _():
+        in_copies[0].start()
+        in_copies[1].start()
+
     weight_copies = []
     pieces = 3
     piece = width // pieces
@@ -162,8 +178,9 @@
         mod_copy(k).start()
 
     span_all = patches * per_dev
+    in_copies[2].wait()
     for kind in range(2):
-        whole = stale_ref[:, kind, :].astype(F32)
+        whole = stale_held[:, kind, :].astype(F32)
         kept = jnp.concatenate(
             [whole[r * span_all + per_dev:(r + 1) * span_all] for r in range(requests)], axis=0).astype(BF16)
         for d in range(active):
@@ -188,8 +205,8 @@
 
     @pl.when(section == 0)
     def _():
-        x_buf[pl.ds(0, video_rows)] = video_ref[...]
-        x_buf[pl.ds(video_rows, rows - video_rows)] = text_ref[...]
+        in_copies[0].wait()
+        in_copies[1].wait()
 
     def block(j):
         return pl.ds(pl.multiple_of(j * cols, SLAB), cols)
@@ -284,9 +301,9 @@
     for g in range(groups):
         for kind in range(2):
             span = slice(g * GROUP, (g + 1) * GROUP)
-            part = projected[1 + kind, :, span]
-            cache_video[:, kind, span] = part[:video_rows]
-            cache_text[:, kind, span] = part[video_rows:]
+            cache_held[:, kind, span] = projected[1 + kind, :, span]
+    out_copies[2].start()
+    out_copies[3].start()
 
     @when_active
     def _():
@@ -367,8 +384,8 @@
 
         spread_start(result, result_sems, c)
     spread_finish(result, result_sems)
-    hidden_video[...] = result[pl.ds(0, video_rows)]
-    hidden_text[...] = result[pl.ds(video_rows, rows - video_rows)]
+    out_copies[0].start()
+    out_copies[1].start()
 
     @pl.when(section == 0)
     def _():
@@ -379,6 +396,8 @@
     def _():
         spread_sent(x_buf, x_sems)
 
+    for copy in out_copies:
+        copy.wait()
     spread_sent(result, result_sems)
     for k in range(1, n_mp):
         mod_copy(k).wait_send()
@@ -452,8 +471,8 @@
             jax.ShapeDtypeStruct((video_rows, 2, cols), BF16),
             jax.ShapeDtypeStruct((text_rows, 2, cols), BF16),
         ),
-        in_specs=[smem, smem, vmem, vmem, vmem, vmem, hbm, hbm, hbm],
-        out_specs=(vmem,) * 4,
+        in_specs=[smem, smem, vmem] + [hbm] * 6,
+        out_specs=(hbm,) * 4,
         scratch_shapes=[
             pltpu.VMEM(w_mod.shape[1:], BF16),
             pltpu.VMEM((3, width, cols), BF16),
@@ -468,6 +487,8 @@
             pltpu.VMEM((n_seq, rows, padded(3 * share)), BF16),
             pltpu.VMEM((n_seq, rows, padded(share)), BF16),
             pltpu.VMEM((n_seq, rows, padded(share)), BF16),
+            pltpu.VMEM((video_rows, 2, cols), BF16),
+            pltpu.VMEM((rows, 2, cols), BF16),
             pltpu.VMEM((active, stale_rows, padded(2 * share)), BF16),
             pltpu.VMEM((n_seq, stale_rows, padded(2 * share)), BF16),
             pltpu.VMEM((each, keys, HEAD), BF16),
@@ -484,6 +505,7 @@
             dma((2,)), dma((2,)),
             dma((2, 3)), dma((2, 3)),
             dma((2, 3)), dma((2, 3)),
+            dma((3,)), dma((4,)),
         ],
         compiler_params=pltpu.CompilerParams(
             collective_id=0, has_side_effects=True, vmem_limit_bytes=56 * 1024 * 1024

time: 76.7 us -> 76.4 us (level)
  no operation moved by 1% of the time
where the time goes in v5:
time: 76.4 us; the launch traced here: 76.2 us
  Pallas kernels  74.2 us (97%)
  between operations  1.29 us (2%)
    pallas_call x1, Pallas kernels, body(): pl.pallas_call(functools.partial(kernel, dims), out_shape=(jax.ShapeDtype...  72.3 us
    pallas_call x1, Pallas kernels, body(): pl.pallas_call(store_kernel, out_shape=tuple((jax.ShapeDtypeStruct(o.shap...  1.91 us

profile of v5, /device:TPU:3, one launch (start us, length us, event | category | flops | bytes accessed | tf_op | source)
XLA Modules:
  0.0 76.2 jit_solution(14282467682502655614)
XLA Ops:
  1.3 0.6 fusion.act_ref
  1.9 72.3 %layer.1 = (bf16[64,3072]{1,0:T(8,128)(2,1)}, bf16[16,3072]{1,0:T(8,128)(2,1)}, bf16[64,2,768]{2,1,0:T(2,128)(2,1)}, bf16[16,2,768]{2,1,0:T(2,128)(2,1)}) custom-call(s32[2,4]{1,0:T(2,128)} %lengths_ref.1, s32[2]{0:T(128)} %text_len_ref.1, bf16[1,512]{1,0:T(2,128)(2,1)} %fusion.act_ref, bf16[64,3072]{1,0:T(8,128)(2,1)} %bitcast.18, ...), custom_call_target="tpu_custom_call" | custom-call | flops 1509949440 | bytes 22020096 | tf_op jit(solution)/shard_map/layer/pallas_call | solution.py:466
  74.3 1.9 %store.1 = (bf16[64,3072]{1,0:T(8,128)(2,1)}, bf16[16,3072]{1,0:T(8,128)(2,1)}, bf16[64,2,768]{2,1,0:T(2,128)(2,1)}, bf16[16,2,768]{2,1,0:T(2,128)(2,1)}) custom-call(bf16[64,3072]{1,0:T(8,128)(2,1)} %get-tuple-element.12.refs_0_, bf16[16,3072]{1,0:T(8,128)(2,1)} %get-tuple-element.13.refs_1_, bf16[64,2,768]{2,1,0:T(2,128)(2,1)} %get-tuple-element.14.refs_2_, ...), custom_call_target="tpu_custom_call" | custom-call | tf_op jit(solution)/shard_map/store/pallas_call | solution.py:522
  (1 shorter events, 0.0 us)

commit v6 on v5

--- a/solution.py
+++ b/solution.py
@@ -84,7 +84,7 @@
     mod_piece = w_mod.shape[0] // mod_pieces
     mod_weights = [
         pltpu.make_async_copy(w_mod_hbm.at[pl.ds(i * mod_piece, mod_piece)], w_mod.at[pl.ds(i * mod_piece, mod_piece)],
-                              w_sem.at[11 + i]) for i in range(mod_pieces)]
+                              w_sem.at[3 * groups + 1 + i]) for i in range(mod_pieces)]
     for copy in mod_weights:
         copy.start()
     in_copies = [
@@ -104,15 +104,14 @@
         in_copies[1].start()
 
     weight_copies = []
-    pieces = 3
-    piece = width // pieces
-    for part in (1, 2, 0):
-        for i in range(pieces):
+    tile_order = sorted(range(groups), key=lambda g: min(g, groups - 1 - g))
+    for g in tile_order:
+        for part in range(3):
             weight_copies.append(pltpu.make_async_copy(
-                w_qkv_hbm.at[part, pl.ds(i * piece, piece)],
-                w_qkv.at[part, pl.ds(i * piece, piece)],
-                w_sem.at[1 + part * pieces + i]))
-    weight_copies.append(pltpu.make_async_copy(w_out_hbm, w_out, w_sem.at[1 + 3 * pieces]))
+                w_qkv_hbm.at[part, :, pl.ds(g * GROUP, GROUP)],
+                w_qkv.at[g, :, pl.ds(part * GROUP, GROUP)],
+                w_sem.at[g * 3 + part]))
+    weight_copies.append(pltpu.make_async_copy(w_out_hbm, w_out, w_sem.at[3 * groups]))
     barrier = pltpu.get_barrier_semaphore()
     for k in range(1, n_mp):
         pl.semaphore_signal(barrier, inc=1, device_id=at(section, seq, lax.rem(mp + k, n_mp)), device_id_type=MESH)
@@ -262,8 +261,8 @@
         piece_values = (x_buf[:, span].astype(F32) - mean) * inverse
         normed[:, span] = (piece_values * (1.0 + modulated(n_mp + c)) + modulated(c)).astype(BF16)
 
-    def project(part, g):
-        return jnp.dot(normed[...], w_qkv[part, :, g * GROUP:(g + 1) * GROUP], preferred_element_type=F32)
+    def project(g):
+        return jnp.dot(normed[...], w_qkv[g], preferred_element_type=F32)
 
     middle = (n_seq + 1) // 2
     lower = 1 - seq // middle
@@ -271,11 +270,12 @@
     def project_all(order):
         done, sent = set(), set()
         for g in order:
-            for index, part in enumerate((1, 2, 0)):
-                if g == order[0]:
-                    for copy in weight_copies[index * pieces:(index + 1) * pieces]:
-                        copy.wait()
-                tile = project(part, g).astype(BF16)
+            first_copy = 3 * tile_order.index(g)
+            for copy in weight_copies[first_copy:first_copy + 3]:
+                copy.wait()
+            product = project(g)
+            for part in range(3):
+                tile = product[:, part * GROUP:(part + 1) * GROUP].astype(BF16)
                 if part == 0:
                     tile = (tile.astype(F32) * HEAD ** (-0.5)).astype(BF16)
                 projected[part, :, g * GROUP:(g + 1) * GROUP] = tile
@@ -475,7 +475,7 @@
         out_specs=(hbm,) * 4,
         scratch_shapes=[
             pltpu.VMEM(w_mod.shape[1:], BF16),
-            pltpu.VMEM((3, width, cols), BF16),
+            pltpu.VMEM((cols // GROUP, width, 3 * GROUP), BF16),
             pltpu.VMEM((cols, width), BF16),
             pltpu.VMEM((rows, width), BF16),
             pltpu.VMEM((rows, width), BF16),
@@ -496,7 +496,7 @@
             pltpu.VMEM((3, rows, cols), BF16),
             pltpu.VMEM((3, rows, cols), BF16),
             pltpu.VMEM((rows, keys), F32),
-            dma((15,)),
+            dma((3 * (cols // GROUP) + 5,)),
             dma((n_mp,)), dma((n_mp,)),
             dma((n_seq,)), dma((n_seq,)),
             dma((n_seq,)), dma((n_seq,)),

time: 76.4 us -> 75.4 us (0.987)
  Pallas kernels: 74.2 us -> 73.2 us
    pallas_call x1, Pallas kernels: 72.3 us -> 71.3 us  [body(): pl.pallas_call(functools.partial(kernel, dims), out_shape=(jax.ShapeDtype...]
where the time goes in v6:
time: 75.4 us; the launch traced here: 75.2 us
  Pallas kernels  73.2 us (97%)
  between operations  1.29 us (2%)
    pallas_call x1, Pallas kernels, body(): pl.pallas_call(functools.partial(kernel, dims), out_shape=(jax.ShapeDtype...  71.3 us
    pallas_call x1, Pallas kernels, body(): pl.pallas_call(store_kernel, out_shape=tuple((jax.ShapeDtypeStruct(o.shap...  1.91 us

profile of v6, /device:TPU:3, one launch (start us, length us, event | category | flops | bytes accessed | tf_op | source)
XLA Modules:
  0.0 75.2 jit_solution(16865884995940485211)
XLA Ops:
  1.3 0.6 fusion.act_ref
  1.9 71.3 %layer.1 = (bf16[64,3072]{1,0:T(8,128)(2,1)}, bf16[16,3072]{1,0:T(8,128)(2,1)}, bf16[64,2,768]{2,1,0:T(2,128)(2,1)}, bf16[16,2,768]{2,1,0:T(2,128)(2,1)}) custom-call(s32[2,4]{1,0:T(2,128)} %lengths_ref.1, s32[2]{0:T(128)} %text_len_ref.1, bf16[1,512]{1,0:T(2,128)(2,1)} %fusion.act_ref, bf16[64,3072]{1,0:T(8,128)(2,1)} %bitcast.18, ...), custom_call_target="tpu_custom_call" | custom-call | flops 1509949440 | bytes 22020096 | tf_op jit(solution)/shard_map/layer/pallas_call | solution.py:466
  73.3 1.9 %store.1 = (bf16[64,3072]{1,0:T(8,128)(2,1)}, bf16[16,3072]{1,0:T(8,128)(2,1)}, bf16[64,2,768]{2,1,0:T(2,128)(2,1)}, bf16[16,2,768]{2,1,0:T(2,128)(2,1)}) custom-call(bf16[64,3072]{1,0:T(8,128)(2,1)} %get-tuple-element.12.refs_0_, bf16[16,3072]{1,0:T(8,128)(2,1)} %get-tuple-element.13.refs_1_, bf16[64,2,768]{2,1,0:T(2,128)(2,1)} %get-tuple-element.14.refs_2_, ...), custom_call_target="tpu_custom_call" | custom-call | tf_op jit(solution)/shard_map/store/pallas_call | solution.py:522
  (1 shorter events, 0.0 us)
